TPU v7x, 512 devices: a whole 4x8x8 slice. The times are simulated.
512 devices in a mesh: ctx: 64 (over z, x, core), kvh: 8 (over y).
Axes of the slice: x: 4, y: 8, z: 8, core: 2. Of those that a mesh axis runs over, the one named last changes fastest.
Arguments:
- tokens: bfloat16 [2, 4, 8192], P(None, None, 'ctx'), may hold values from -6 to 6
- lengths: int32 [4], replicated, may hold values from 4096 to 16384, as said below
- attn_gain: bfloat16 [8192], P('ctx'), may hold values from 0.25 to 1.75
- ffn_gain: bfloat16 [8192], P('ctx'), may hold values from 0.25 to 1.75
- w_q: bfloat16 [8192, 8192], P('ctx', 'kvh'), may hold values from -5 to 5
- w_k: bfloat16 [8192, 1024], P('ctx', 'kvh'), may hold values from -0.25 to 0.25
- w_v: bfloat16 [8192, 1024], P('ctx', 'kvh'), may hold values from -0.25 to 0.25
- w_o: bfloat16 [8192, 8192], P('kvh', 'ctx'), may hold values from -0.0625 to 0.0625
- w_gate: bfloat16 [8192, 28672], P('ctx', 'kvh'), may hold values from -0.0625 to 0.0625
- w_up: bfloat16 [8192, 28672], P('ctx', 'kvh'), may hold values from -0.0625 to 0.0625
- w_down: bfloat16 [28672, 8192], P('kvh', 'ctx'), may hold values from -0.03125 to 0.03125
- k_cache: bfloat16 [4, 16384, 8, 128], P(None, 'ctx', 'kvh'), may hold values from -112 to 112
- v_cache: bfloat16 [4, 16384, 8, 128], P(None, 'ctx', 'kvh'), may hold values from -6 to 6
Outputs:
- attended: bfloat16 [2, 4, 8192], P(None, None, 'ctx')
- layer_out: bfloat16 [2, 4, 8192], P(None, None, 'ctx')
Inputs may be any that keep to these rules, and one draw needn't show every extreme that they name: `lengths`: every length is at least 4096, and some request has exactly 16384.
All inputs are finite; a program needn't handle non-finite values.
Results may differ from a plain program's by a relative error of at most 0.015.
Values may be sent and summed in bfloat16 or wider, within the bound.
A program may use at most 64 MiB of HBM per device.

v0:
```python
import math

import jax
import jax.numpy as jnp
from jax import lax
from jax.sharding import PartitionSpec as P

D = 8192
H = 64
KVH = 8


eps_value = 1e-05


def merged(value, axis, join):
    pieces = jax.tree.map(lambda part: lax.all_gather(part, axis), value)
    head = jax.tree.map(lambda part: part[0], pieces)
    tail = jax.tree.map(lambda part: part[1:], pieces)
    so_far, _ = lax.scan(lambda so_far, piece: (join(so_far, piece), None), head, tail)
    return so_far


def rotary(values, position):
    half = values.shape[-1] // 2
    freq = 500000.0 ** (-(jnp.arange(half).astype(jnp.float32) * 2.0) / values.shape[-1])
    angle = position[..., None].astype(jnp.float32) * freq
    cosine = jnp.cos(angle)
    sine = jnp.sin(angle)
    first = values[..., :half]
    second = values[..., half:]
    return jnp.concatenate(
        [first * cosine - second * sine, second * cosine + first * sine], axis=-1
    )


def combine_parts(left, right):
    high_a, total_a, acc_a = left
    high_b, total_b, acc_b = right
    peak = jnp.maximum(high_a, high_b)
    factor_a = jnp.exp(high_a - peak)
    factor_b = jnp.exp(high_b - peak)
    return (
        peak,
        total_a * factor_a + total_b * factor_b,
        acc_a * factor_a[..., None] + acc_b * factor_b[..., None],
    )


def finish(high, total, acc, fresh, fresh_vals):
    top = jnp.maximum(high, jnp.max(fresh, -1))
    factor = jnp.exp(high - top)
    fresh_w = jnp.exp(fresh - top[..., None])
    whole = total * factor + jnp.sum(fresh_w, -1)
    summed = acc * factor[..., None] + jnp.einsum(
        "bgrj,bgjd->bgrd",
        fresh_w.astype(jnp.bfloat16),
        fresh_vals,
        preferred_element_type=jnp.float32,
    )
    return summed / whole[..., None]


def body(
    tokens, lengths, attn_gain, ffn_gain, w_q, w_k, w_v, w_o, w_gate, w_up, w_down, k_cache, v_cache
):
    batch = tokens.shape[1]
    span = k_cache.shape[1]
    groups = k_cache.shape[2]
    head_dim = k_cache.shape[3]
    ratio = H // KVH
    positions = lax.axis_index("ctx") * span + jnp.arange(span)
    valid = (positions[None, :] < lengths[:, None])[:, None, None, :]
    new_keys = []
    new_values = []
    attended_list = []
    output_list = []
    for step in range(2):
        x = tokens[step].astype(jnp.float32)
        sq_local = jnp.sum(x * x, -1)
        xg = (x * attn_gain.astype(jnp.float32)).astype(jnp.bfloat16)
        q_part = jnp.dot(xg, w_q, preferred_element_type=jnp.float32)
        k_part = jnp.dot(xg, w_k, preferred_element_type=jnp.float32)
        v_part = jnp.dot(xg, w_v, preferred_element_type=jnp.float32)
        sq_attn, q_sum, k_sum, v_sum = lax.psum((sq_local, q_part, k_part, v_part), "ctx")
        scale_a = lax.rsqrt(sq_attn / D + eps_value)[:, None]
        q_full = q_sum * scale_a
        k_full = k_sum * scale_a
        v_full = v_sum * scale_a
        position = lengths + step
        queries = (
            rotary(q_full.reshape(batch, groups * ratio, head_dim), position[:, None])
            .astype(jnp.bfloat16)
            .reshape(batch, groups, ratio, head_dim)
        )
        new_keys.append(
            rotary(k_full.reshape(batch, groups, head_dim), position[:, None]).astype(jnp.bfloat16)
        )
        new_values.append(v_full.reshape(batch, groups, head_dim).astype(jnp.bfloat16))
        fresh_k = jnp.stack(new_keys, 2)
        fresh_v = jnp.stack(new_values, 2)
        scores = jnp.einsum(
            "bgrd,bpgd->bgrp", queries, k_cache, preferred_element_type=jnp.float32
        ) / math.sqrt(head_dim)
        scores = jnp.where(valid, scores, -1e30)
        high = jnp.max(scores, -1)
        weights = jnp.where(valid, jnp.exp(scores - high[..., None]), 0.0)
        total = jnp.sum(weights, -1)
        acc = jnp.einsum(
            "bgrp,bpgd->bgrd",
            weights.astype(jnp.bfloat16),
            v_cache,
            preferred_element_type=jnp.float32,
        )
        fresh = jnp.einsum(
            "bgrd,bgjd->bgrj", queries, fresh_k, preferred_element_type=jnp.float32
        ) / math.sqrt(head_dim)
        high_all, total_all, acc_all = merged((high, total, acc), "ctx", combine_parts)
        attn = finish(high_all, total_all, acc_all, fresh, fresh_v).astype(jnp.bfloat16)
        out_part = jnp.dot(attn.reshape(batch, -1), w_o, preferred_element_type=jnp.float32)
        attended = lax.psum(out_part, "kvh")
        x_mid = x + attended
        sq_mid = jnp.sum(x_mid * x_mid, -1)
        xh = (x_mid * ffn_gain.astype(jnp.float32)).astype(jnp.bfloat16)
        gate_part = jnp.dot(xh, w_gate, preferred_element_type=jnp.float32)
        up_part = jnp.dot(xh, w_up, preferred_element_type=jnp.float32)
        sq_ffn, gate_sum, up_sum = lax.psum((sq_mid, gate_part, up_part), "ctx")
        scale_f = lax.rsqrt(sq_ffn / D + eps_value)[:, None]
        hidden = (jax.nn.silu(gate_sum * scale_f) * (up_sum * scale_f)).astype(jnp.bfloat16)
        down_part = jnp.dot(hidden, w_down, preferred_element_type=jnp.float32)
        ffn_out = lax.psum(down_part, "kvh")
        attended_list.append(attended.astype(jnp.bfloat16))
        output_list.append((x_mid + ffn_out).astype(jnp.bfloat16))
    return (jnp.stack(attended_list, 0), jnp.stack(output_list, 0))


def solution(mesh):
    return jax.shard_map(
        body,
        mesh=mesh,
        in_specs=(
            P(None, None, "ctx"),
            P(),
            P("ctx"),
            P("ctx"),
            P("ctx", "kvh"),
            P("ctx", "kvh"),
            P("ctx", "kvh"),
            P("kvh", "ctx"),
            P("ctx", "kvh"),
            P("ctx", "kvh"),
            P("kvh", "ctx"),
            P(None, "ctx", "kvh", None),
            P(None, "ctx", "kvh", None),
        ),
        out_specs=(P(None, None, "ctx"), P(None, None, "ctx")),
        check_vma=False,
    )
```

profile of v0, /device:TPU:1, one launch (start us, length us, event | category | flops | bytes accessed | tf_op | source)
XLA Modules:
  0.0 976.0 jit_solution(13158298618941915043)
XLA Ops:
  7.3 0.7 convert_element_type.137
  8.0 0.8 fusion.75
  8.8 0.7 add_convert_fusion.4
  9.5 0.8 broadcast_compare_fusion
  10.3 0.9 fusion.112
  11.3 1.1 fusion.114
  12.4 252.8 %all-reduce.2 = (f32[4,1024]{1,0:T(4,128)S(1)}, f32[4]{0:T(128)S(1)}, f32[4,128]{1,0:T(4,128)S(1)}, f32[4,128]{1,0:T(4,128)S(1)}) all-reduce(f32[4,1024]{1,0:T(4,128)S(1)} %fusion.114, f32[4]{0:T(128)S(1)} %fusion.75, f32[4,128]{1,0:T(4,128)S(1)} %fusion.112, f32[4,128]{1,0:T(4,128)S(1)} %fusion.110), channel_id=1, replica_groups=mesh['ctx'=64,'kvh'=8] {'ctx'}, use_global_device_ids=true, to_apply=%region_0.0 | all-reduce | flops 5124 | bytes 40992 | tf_op jit(solution)/shard_map/psum | solution.py:85
  265.5 0.3 fusion.118
  265.8 0.8 fusion.18
  266.7 0.2 fusion.35
  266.9 0.7 copy-done.14
  267.5 51.9 %all-gather.7 = f32[64,4,8]{2,1,0:T(4,128)S(1)} all-gather(f32[1,4,8]{2,1,0:T(4,128)S(1)} %bitcast.302), channel_id=3, replica_groups=mesh['ctx'=64,'kvh'=8] {'ctx'}, dimensions={0}, use_global_device_ids=true | all-gather | bytes 8320 | tf_op jit(solution)/shard_map/all_gather | solution.py:17
  319.4 49.5 %all-gather.6 = f32[64,4,8]{2,1,0:T(4,128)S(1)} all-gather(f32[1,4,8]{2,1,0:T(4,128)S(1)} %bitcast.295), channel_id=2, replica_groups=mesh['ctx'=64,'kvh'=8] {'ctx'}, dimensions={0}, use_global_device_ids=true | all-gather | bytes 8320 | tf_op jit(solution)/shard_map/all_gather | solution.py:17
  369.1 0.2 fusion.86
  369.3 0.3 copy-done.6
  369.9 0.9 copy-done.4
  370.9 0.1 fusion.108
  371.0 0.7 slice_bitcast_fusion.5
  371.7 1.3 slice-done.1
  373.0 7.9 while.28
  381.0 0.1 fusion.51
  381.2 13.9 %psum.130 = f32[4,128]{1,0:T(4,128)S(1)} all-reduce(f32[4,128]{1,0:T(4,128)S(1)} %fusion.51), channel_id=1, replica_groups=mesh['ctx'=64,'kvh'=8] {'kvh'}, use_global_device_ids=true, to_apply=%region_9.10 | all-reduce | flops 512 | bytes 4096 | tf_op jit(solution)/shard_map/psum | solution.py:121
  395.1 0.6 multiply_reduce_fusion.1
  395.7 244.4 %all-reduce.1 = (f32[4,1024]{1,0:T(4,128)S(1)}, f32[4]{0:T(128)S(1)}, f32[4,128]{1,0:T(4,128)S(1)}, f32[4,128]{1,0:T(4,128)S(1)}) all-reduce(f32[4,1024]{1,0:T(4,128)S(1)} %fusion.108, f32[4]{0:T(128)S(1)} %get-tuple-element.115, f32[4,128]{1,0:T(4,128)S(1)} %fusion.106, ...), channel_id=1, replica_groups=mesh['ctx'=64,'kvh'=8] {'ctx'}, use_global_device_ids=true, to_apply=%region_10.11 | all-reduce | flops 5124 | bytes 40992 | tf_op jit(solution)/shard_map/psum | solution.py:85
  640.2 0.3 fusion.119
  640.5 0.2 fusion.37
  640.7 0.8 fusion.16
  641.6 52.1 %all-gather.9 = f32[64,4,8]{2,1,0:T(4,128)S(1)} all-gather(f32[1,4,8]{2,1,0:T(4,128)S(1)} %bitcast.301), channel_id=6, replica_groups=mesh['ctx'=64,'kvh'=8] {'ctx'}, dimensions={0}, use_global_device_ids=true | all-gather | bytes 8320 | tf_op jit(solution)/shard_map/all_gather | solution.py:17
  693.6 49.5 %all-gather.8 = f32[64,4,8]{2,1,0:T(4,128)S(1)} all-gather(f32[1,4,8]{2,1,0:T(4,128)S(1)} %bitcast.296), channel_id=5, replica_groups=mesh['ctx'=64,'kvh'=8] {'ctx'}, dimensions={0}, use_global_device_ids=true | all-gather | bytes 8320 | tf_op jit(solution)/shard_map/all_gather | solution.py:17
  743.4 0.2 fusion.120
  743.7 0.9 fusion.122
  744.5 0.9 fusion.121
  745.4 0.7 slice_bitcast_fusion.4
  746.1 1.2 slice-done
  747.3 7.9 while.29
  755.3 0.2 fusion.15
  755.4 0.2 fusion.48
  755.6 11.5 %psum.135 = f32[4,128]{1,0:T(4,128)S(1)} all-reduce(f32[4,128]{1,0:T(4,128)S(1)} %fusion.48), channel_id=1, replica_groups=mesh['ctx'=64,'kvh'=8] {'kvh'}, use_global_device_ids=true, to_apply=%region_21.22 | all-reduce | flops 512 | bytes 4096 | tf_op jit(solution)/shard_map/psum | solution.py:121
  767.1 0.6 multiply_reduce_fusion
  767.7 0.9 fusion.124
  768.5 0.8 fusion.123
  769.4 183.4 %all-reduce.6.cloned.1.call-done = (f32[4,3584]{1,0:T(4,128)}, f32[4,3584]{1,0:T(4,128)}, f32[4]{0:T(128)}, f32[4,3584]{1,0:T(4,128)}, f32[4,3584]{1,0:T(4,128)}, /*index=5*/f32[4]{0:T(128)}) async-done(((f32[4,3584]{1,0:T(4,128)}, f32[4,3584]{1,0:T(4,128)}, f32[4]{0:T(128)}, f32[4,3584]{1,0:T(4,128)}, f32[4,3584]{1,0:T(4,128)}, /*index=5*/f32[4]{0:T(128)}), (f32[4,3584]{1,0:T(4,128)}, f32[4,3584]{1,0:T(4,128)}, ...) | async-done | bytes 229424 | tf_op jit(solution)/shard_map/psum | solution.py:127
  952.8 0.6 copy-done.9
  953.5 1.2 fusion.26
  954.7 0.3 fusion.28
  955.0 13.2 %all-reduce.3 = (f32[4,128]{1,0:T(4,128)S(1)}, f32[4,128]{1,0:T(4,128)S(1)}) all-reduce(f32[4,128]{1,0:T(4,128)S(1)} %fusion.28, f32[4,128]{1,0:T(4,128)S(1)} %fusion.26), channel_id=1, replica_groups=mesh['ctx'=64,'kvh'=8] {'kvh'}, use_global_device_ids=true, to_apply=%region_31.32 | all-reduce | flops 1024 | bytes 8192 | tf_op jit(solution)/shard_map/psum | solution.py:131
  968.3 0.6 pad_maximum_fusion.3
  968.9 0.6 pad_maximum_fusion.2
  (578 shorter events, 16.2 us)
Async XLA Ops:
  7.2 736.5 %copy-start = (bf16[128,3584]{1,0:T(8,128)(2,1)S(1)}, bf16[128,3584]{1,0:T(8,128)(2,1)}, u32[]{:S(2)}) copy-start(bf16[128,3584]{1,0:T(8,128)(2,1)} %param.26) | copy-start | bytes 2752516
  7.2 4.0 copy-start.7
  7.2 363.8 %all-gather.13.cloned.1.call-start = ((), (), s32[]{:S(2)}) async-start(), calls=%async_computation | async-start | bytes 1064960 | tf_op jit(solution)/shard_map/all_gather | solution.py:17
  8.8 2.4 copy-start.8
  9.5 256.0 %copy-start.2 = (bf16[4,256,1,128]{3,1,2,0:T(8,128)(2,1)S(1)}, bf16[4,256,1,128]{3,1,2,0:T(8,128)(2,1)}, u32[]{:S(2)}) copy-start(bf16[4,256,1,128]{3,1,2,0:T(8,128)(2,1)} %param.28) | copy-start | bytes 786436
  12.4 253.3 %copy-start.3 = (bf16[4,256,1,128]{3,1,2,0:T(8,128)(2,1)S(1)}, bf16[4,256,1,128]{3,1,2,0:T(8,128)(2,1)}, u32[]{:S(2)}) copy-start(bf16[4,256,1,128]{3,1,2,0:T(8,128)(2,1)} %param.29) | copy-start | bytes 786436
  266.7 478.7 %all-gather.15.cloned.1.call-start = ((), (), s32[]{:S(2)}) async-start(), calls=%async_computation.1 | async-start | bytes 1064960 | tf_op jit(solution)/shard_map/all_gather | solution.py:17
  266.9 0.7 copy-start.14
  368.9 0.8 copy-start.6
  369.9 1.0 copy-start.4
  371.7 1.3 slice-start.1
  371.7 9.3 copy-start.5
  641.5 311.3 %all-reduce.6.cloned.1.call-start = ((), (), s32[]{:S(2)}) async-start(), calls=%async_computation.2 | async-start | bytes 460800 | tf_op jit(solution)/shard_map/psum | solution.py:127
  641.6 102.9 %copy-start.1 = (bf16[128,3584]{1,0:T(8,128)(2,1)S(1)}, bf16[128,3584]{1,0:T(8,128)(2,1)}, u32[]{:S(2)}) copy-start(bf16[128,3584]{1,0:T(8,128)(2,1)} %param.25) | copy-start | bytes 2752516
  746.1 1.2 slice-start
  767.7 185.8 %copy-start.11 = (bf16[3584,128]{1,0:T(8,128)(2,1)S(1)}, bf16[3584,128]{1,0:T(8,128)(2,1)}, u32[]{:S(2)}) copy-start(bf16[3584,128]{1,0:T(8,128)(2,1)} %param.27) | copy-start | bytes 2752516
  952.8 0.6 copy-start.9
  952.8 0.7 copy-start.10
  953.5 1.2 copy-start.12
  953.5 1.2 copy-start.13
Sparse Core Ops, SparseCore 0:
  266.8 81.5 all-gather.12
  641.7 79.4 all-gather.14
  769.5 183.2 all-reduce.5
where the time goes:
time: 979 us; the launch traced here: 976 us
  blocking collectives  739 us (75%)
  waiting for transfers between devices  183 us (19%)
  other arithmetic  20.9 us (2%)
  between operations  14 us (1%)
  matrix products  10.5 us (1%)
    psum x2, blocking collectives, body(): lax.psum((sq_local, q_part, k_part, v_part), 'ctx')  497 us
    all_gather x4, blocking collectives, merged(): pieces = jax.tree.map(lambda part: lax.all_gather(part, axis), value)  203 us
    psum x1, waiting for transfers between devices, body(): sq_ffn, gate_sum, up_sum = lax.psum((sq_mid, gate_part, up_part), 'ctx')  183 us
    psum x2, blocking collectives, body(): attended = lax.psum(out_part, 'kvh')  25.4 us
  transfers between devices with their start and end apart: 3, of which 1 were waited for; matrix products, arithmetic and copies ran while one was open for 0% of the time, Pallas kernels for 0%

commit v1 on v0

v1 whole, which is shorter than its diff:
```python
import math

import jax
import jax.numpy as jnp
import numpy as np
from jax import lax
from jax.experimental import pallas as pl
from jax.experimental.pallas import tpu as pltpu
from jax.sharding import PartitionSpec as P

MESH = pl.DeviceIdType.MESH
D = 8192
EPS = 1e-05
F32 = jnp.float32
BF16 = jnp.bfloat16
FAR_FIRST = (4, 3, 5, 2, 6, 1, 7)
TILES = 28
BLOCK = 512
QKV_RS, QKV_AR, QKV_AG, ATT_RS, ATT_AR, ATT_AG, OUT_AR, SQ_RS, FFN_RS, SQ_AR, FFN_AR, FFN_AG, DOWN_AR = range(13)


def total_of(ref, rows):
    parts = [ref[i, rows, :].astype(F32) for i in range(8)]
    return ((parts[0] + parts[1]) + (parts[2] + parts[3])) + (
        (parts[4] + parts[5]) + (parts[6] + parts[7])
    )


def row_of(column):
    lane = lax.broadcasted_iota(jnp.int32, (8, 128), 1)
    row = lax.broadcasted_iota(jnp.int32, (8, 128), 0)
    return jnp.sum(jnp.where(lane == row, column, 0.0), axis=0, keepdims=True)


def column_of(line):
    lane = lax.broadcasted_iota(jnp.int32, (8, 128), 1)
    row = lax.broadcasted_iota(jnp.int32, (8, 128), 0)
    return jnp.sum(jnp.where(lane == row, line, 0.0), axis=1, keepdims=True)


def merged(ref):
    lane = lax.broadcasted_iota(jnp.int32, (8, 128), 1)
    low = lane < 64
    peaks, totals = [], []
    for i in range(8):
        both = ref[i, 8:16, :]
        turned = pltpu.roll(both, 64, 1)
        peaks.append(jnp.where(low, both, turned))
        totals.append(jnp.where(low, turned, both))
    peak = peaks[0]
    for i in range(1, 8):
        peak = jnp.maximum(peak, peaks[i])
    total = jnp.zeros((8, 128), F32)
    summed = jnp.zeros((8, 128), F32)
    for i in range(8):
        factor = jnp.exp(peaks[i] - peak)
        total += factor * totals[i]
        summed += factor * ref[i, 0:8, :]
    return peak, total, summed


def kernel(
    lengths, tokens, attn_gain, ffn_gain, freq,
    h_q, h_k, h_v, h_o, h_gate, h_up, h_down, h_kc, h_vc,
    attended_ref, layer_ref,
    w_q, w_k, w_v, w_o, w_gate, w_up, w_down, k_c, v_c,
    s_qkv, r_qkv, r_qkv2, r_q,
    heads, sums, peaks,
    s_att, r_att, r_att2, r_attn,
    r_out,
    s_sq, r_sq, r_sq2,
    s_ffn, r_ffn, r_ffn2, r_hid,
    r_down,
    load_sem, send_sem, recv_sem,
):
    ctx = lax.axis_index("ctx")
    kvh = lax.axis_index("kvh")
    xc = lax.rem(ctx, 8)
    z = ctx // 8

    def xc_peer(d):
        to = lax.rem(xc + d, 8)
        return to, (z * 8 + to, kvh)

    def z_peer(d):
        return (lax.rem(z + d, 8) * 8 + xc, kvh)

    def y_peer(d):
        return (ctx, lax.rem(kvh + d, 8))

    def send(src, dst, stage, peer):
        pltpu.make_async_remote_copy(
            src_ref=src, dst_ref=dst, send_sem=send_sem.at[stage], recv_sem=recv_sem.at[stage],
            device_id=peer, device_id_type=MESH,
        ).start()

    def arrived(ref, stage):
        pltpu.make_async_copy(ref, ref, recv_sem.at[stage]).wait()

    loads = {}
    for i, (name, src, dst) in enumerate(
        (
            ("q", h_q, w_q), ("k", h_k, w_k), ("v", h_v, w_v), ("kc", h_kc, k_c), ("vc", h_vc, v_c),
            ("o", h_o, w_o), ("gate", h_gate, w_gate), ("up", h_up, w_up), ("down", h_down, w_down),
        )
    ):
        loads[name] = pltpu.make_async_copy(src, dst, load_sem.at[i])
        loads[name].start()

    barrier = pltpu.get_barrier_semaphore()
    for d in FAR_FIRST:
        for peer in (z_peer(d), y_peer(d), xc_peer(d)[1]):
            pl.semaphore_signal(barrier, inc=1, device_id=peer, device_id_type=MESH)

    x = jnp.concatenate([tokens[0], tokens[1]], axis=0).astype(F32)
    sq = row_of(jnp.sum(x * x, axis=1, keepdims=True))
    xg = (x * attn_gain[...].astype(F32)).astype(BF16)
    for name in ("q", "k", "v"):
        loads[name].wait()
    q_part = jnp.dot(xg, w_q[...], preferred_element_type=F32)
    k_part = jnp.dot(xg, w_k[...], preferred_element_type=F32)
    v_part = jnp.dot(xg, w_v[...], preferred_element_type=F32)
    sq_tile = jnp.broadcast_to(sq, (8, 128))
    for j in range(8):
        s_qkv[j, 0:8, :] = q_part[:, j * 128 : (j + 1) * 128]
        s_qkv[j, 8:16, :] = k_part if j < 4 else v_part
        s_qkv[j, 16:24, :] = sq_tile
    r_qkv[xc] = s_qkv[xc]

    pl.semaphore_wait(barrier, 21)
    for d in FAR_FIRST:
        to, peer = xc_peer(d)
        send(s_qkv.at[to, pl.ds(0, 17)], r_qkv.at[xc, pl.ds(0, 17)], QKV_RS, peer)

    row = lax.broadcasted_iota(jnp.int32, (8, 128), 0)
    lane = lax.broadcasted_iota(jnp.int32, (8, 128), 1)
    position = jnp.where(row >= 4, 1, 0)
    for b in range(4):
        position += jnp.where(lax.rem(row, 4) == b, lengths[b], 0)
    angle = position.astype(F32) * freq[...]
    cosine = jnp.cos(angle)
    sine = jnp.sin(angle)
    sine = jnp.where(lane < 64, -sine, sine)

    def rotary(a):
        return a * cosine + pltpu.roll(a, 64, 1) * sine

    arrived(r_qkv.at[pl.ds(0, 7), pl.ds(0, 17)], QKV_RS)
    r_qkv2[z, 0:16, :] = total_of(r_qkv, pl.ds(0, 16))
    r_qkv2[z, 16:17, :] = total_of(r_qkv, pl.ds(16, 1))
    for d in FAR_FIRST:
        mine = r_qkv2.at[z, pl.ds(0, 17)]
        send(mine, mine, QKV_AR, z_peer(d))
    arrived(r_qkv2.at[pl.ds(0, 7), pl.ds(0, 17)], QKV_AR)
    scale = lax.rsqrt(column_of(total_of(r_qkv2, pl.ds(16, 1))) / D + EPS)
    q_mine = rotary(total_of(r_qkv2, pl.ds(0, 8)) * scale).astype(BF16)
    kv_mine = total_of(r_qkv2, pl.ds(8, 8)) * scale
    kv_mine = jnp.where(xc < 4, rotary(kv_mine), kv_mine).astype(BF16)
    r_q[xc] = jnp.concatenate([q_mine, kv_mine], axis=0)
    for d in FAR_FIRST:
        send(r_q.at[xc], r_q.at[xc], QKV_AG, xc_peer(d)[1])
    q_mine = q_mine.astype(F32)
    loads["kc"].wait()
    loads["vc"].wait()
    arrived(r_q.at[pl.ds(0, 7)], QKV_AG)

    for h in range(8):
        heads[h * 8 : (h + 1) * 8, :] = r_q[h].astype(F32)[0:8, :]
    spot = ctx * 256 + lax.broadcasted_iota(jnp.int32, (16, 256), 1)
    low16 = lax.broadcasted_iota(jnp.int32, (16, 128), 1) < 64
    for b in range(4):
        queries = jnp.concatenate(
            [heads[pl.ds(b, 8, stride=8), :], heads[pl.ds(b + 4, 8, stride=8), :]], axis=0
        ).astype(BF16)
        scores = lax.dot_general(
            queries, k_c[b], (((1,), (1,)), ((), ())), preferred_element_type=F32
        ) / math.sqrt(128)
        valid = spot < lengths[b]
        scores = jnp.where(valid, scores, -1e30)
        peak = jnp.max(scores, axis=1, keepdims=True)
        weights = jnp.where(valid, jnp.exp(scores - peak), 0.0)
        total = jnp.sum(weights, axis=1, keepdims=True)
        acc = jnp.dot(weights.astype(BF16), v_c[b], preferred_element_type=F32)
        both = jnp.where(low16, peak, total)
        for s in range(2):
            at = (s * 4 + b) * 8
            sums[at : at + 8, :] = acc[s * 8 : s * 8 + 8, :]
            peaks[at : at + 8, :] = both[s * 8 : s * 8 + 8, :]
    for h in range(8):
        s_att[h, 0:8, :] = sums[pl.ds(h, 8, stride=8), :]
        s_att[h, 8:16, :] = peaks[pl.ds(h, 8, stride=8), :]
    r_att[xc] = s_att[xc]
    for d in FAR_FIRST:
        to, peer = xc_peer(d)
        send(s_att.at[to], r_att.at[xc], ATT_RS, peer)

    k_new = r_q[0].astype(F32)[8:16, :]
    v_new = r_q[4].astype(F32)[8:16, :]
    k_first = jnp.concatenate([k_new[0:4], k_new[0:4]], axis=0)
    k_second = jnp.concatenate([k_new[4:8], k_new[4:8]], axis=0)
    v_first = jnp.concatenate([v_new[0:4], v_new[0:4]], axis=0)
    v_second = jnp.concatenate([v_new[4:8], v_new[4:8]], axis=0)
    f_first = jnp.sum(q_mine * k_first, axis=1, keepdims=True) / math.sqrt(128)
    f_second = jnp.sum(q_mine * k_second, axis=1, keepdims=True) / math.sqrt(128)
    f_first = jnp.broadcast_to(f_first, (8, 128))
    f_second = jnp.broadcast_to(f_second, (8, 128))
    second = row >= 4
    f_second = jnp.where(second, f_second, -1e30)

    arrived(r_att.at[pl.ds(0, 7)], ATT_RS)
    peak, total, summed = merged(r_att)
    r_att2[z, 0:8, :] = summed
    r_att2[z, 8:16, :] = jnp.where(lane < 64, peak, total)
    for d in FAR_FIRST:
        send(r_att2.at[z], r_att2.at[z], ATT_AR, z_peer(d))
    loads["o"].wait()
    arrived(r_att2.at[pl.ds(0, 7)], ATT_AR)
    peak, total, summed = merged(r_att2)
    top = jnp.maximum(peak, jnp.maximum(f_first, f_second))
    factor = jnp.exp(peak - top)
    e_first = jnp.exp(f_first - top)
    e_second = jnp.where(second, jnp.exp(f_second - top), 0.0)
    total = total * factor + e_first + e_second
    summed = (
        summed * factor
        + e_first.astype(BF16).astype(F32) * v_first
        + e_second.astype(BF16).astype(F32) * v_second
    )
    r_attn[xc] = summed / total
    for d in FAR_FIRST:
        send(r_attn.at[xc], r_attn.at[xc], ATT_AG, xc_peer(d)[1])
    arrived(r_attn.at[pl.ds(0, 7)], ATT_AG)

    attn = jnp.concatenate([r_attn[h] for h in range(8)], axis=1).astype(BF16)
    r_out[kvh] = jnp.dot(attn, w_o[...], preferred_element_type=F32)
    for d in FAR_FIRST:
        send(r_out.at[kvh], r_out.at[kvh], OUT_AR, y_peer(d))
    loads["gate"].wait()
    loads["up"].wait()
    arrived(r_out.at[pl.ds(0, 7)], OUT_AR)
    attended = total_of(r_out, pl.ds(0, 8))
    x_mid = x + attended
    s_sq[...] = jnp.broadcast_to(row_of(jnp.sum(x_mid * x_mid, axis=1, keepdims=True)), (8, 128))
    r_sq[xc] = s_sq[...]
    for d in FAR_FIRST:
        send(s_sq.at[pl.ds(0, 1)], r_sq.at[xc, pl.ds(0, 1)], SQ_RS, xc_peer(d)[1])
    attended_ref[0] = attended[0:4].astype(BF16)
    attended_ref[1] = attended[4:8].astype(BF16)

    xh = (x_mid * ffn_gain[...].astype(F32)).astype(BF16)
    for d in FAR_FIRST + (0,):
        to, peer = xc_peer(d)
        start = pl.multiple_of(((to // 2) * 7 + lax.rem(to, 2) * 3) * 128, 128)
        gate = jnp.dot(xh, w_gate[:, pl.ds(start, BLOCK)], preferred_element_type=F32)
        up = jnp.dot(xh, w_up[:, pl.ds(start, BLOCK)], preferred_element_type=F32)
        both = jnp.concatenate([gate, up], axis=0).astype(BF16)
        if d:
            s_ffn[to] = both
            send(s_ffn.at[to], r_ffn.at[xc], FFN_RS, peer)
        else:
            r_ffn[xc] = both
    arrived(r_sq.at[pl.ds(0, 7), pl.ds(0, 1)], SQ_RS)
    r_sq2[z, 0:1, :] = total_of(r_sq, pl.ds(0, 1))
    for d in FAR_FIRST:
        mine = r_sq2.at[z, pl.ds(0, 1)]
        send(mine, mine, SQ_AR, z_peer(d))
    arrived(r_ffn.at[pl.ds(0, 7)], FFN_RS)
    r_ffn2[z] = total_of(r_ffn, pl.ds(0, 16)).astype(BF16)
    for d in FAR_FIRST:
        send(r_ffn2.at[z], r_ffn2.at[z], FFN_AR, z_peer(d))
    arrived(r_sq2.at[pl.ds(0, 7), pl.ds(0, 1)], SQ_AR)
    scale = lax.rsqrt(column_of(total_of(r_sq2, pl.ds(0, 1))) / D + EPS)
    loads["down"].wait()
    arrived(r_ffn2.at[pl.ds(0, 7)], FFN_AR)
    both = total_of(r_ffn2, pl.ds(0, 16))
    gate = both[0:8] * scale
    hidden = gate / (1.0 + jnp.exp(-gate)) * (both[8:16] * scale)
    r_hid[xc] = jnp.concatenate([hidden[:, 0:256], hidden[:, 256:512]], axis=0).astype(BF16)
    for d in FAR_FIRST:
        send(r_hid.at[xc], r_hid.at[xc], FFN_AG, xc_peer(d)[1])
    arrived(r_hid.at[pl.ds(0, 7)], FFN_AG)

    pieces = []
    for j in range(8):
        piece = r_hid[j].astype(F32)
        if j % 2 == 0:
            pieces.append(piece[0:8])
        else:
            pieces.append(piece[0:8, 128:256])
        pieces.append(piece[8:16])
    r_down[kvh] = jnp.dot(
        jnp.concatenate(pieces, axis=1).astype(BF16), w_down[...], preferred_element_type=F32
    )
    for d in FAR_FIRST:
        send(r_down.at[kvh], r_down.at[kvh], DOWN_AR, y_peer(d))
    sent = (
        (r_qkv.at[pl.ds(0, 7), pl.ds(0, 17)], (QKV_RS, QKV_AR)),
        (r_q.at[pl.ds(0, 7)], (QKV_AG,)),
        (r_att.at[pl.ds(0, 7)], (ATT_RS, ATT_AR)),
        (r_attn.at[pl.ds(0, 7)], (ATT_AG, OUT_AR)),
        (r_sq.at[pl.ds(0, 7), pl.ds(0, 1)], (SQ_RS, SQ_AR)),
        (r_ffn.at[pl.ds(0, 7)], (FFN_RS, FFN_AR)),
        (r_hid.at[pl.ds(0, 7)], (FFN_AG,)),
        (r_down.at[pl.ds(0, 7)], (DOWN_AR,)),
    )
    for ref, stages in sent:
        for stage in stages:
            pltpu.make_async_copy(ref, ref, send_sem.at[stage]).wait()
    arrived(r_down.at[pl.ds(0, 7)], DOWN_AR)
    layer = x_mid + total_of(r_down, pl.ds(0, 8))
    layer_ref[0] = layer[0:4].astype(BF16)
    layer_ref[1] = layer[4:8].astype(BF16)


def body(tokens, lengths, attn_gain, ffn_gain, w_q, w_k, w_v, w_o, w_gate, w_up, w_down, k_cache, v_cache):
    half = np.arange(64, dtype=np.float64)
    freq = np.tile(500000.0 ** (-2.0 * half / 128.0), 2).astype(np.float32)[None]
    k_cache = k_cache.reshape(4, 256, 128)
    v_cache = v_cache.reshape(4, 256, 128)
    vmem = pl.BlockSpec(memory_space=pltpu.VMEM)
    hbm = pl.BlockSpec(memory_space=pl.ANY)
    weights = (w_q, w_k, w_v, w_o, w_gate, w_up, w_down, k_cache, v_cache)
    out = jax.ShapeDtypeStruct((2, 4, 128), BF16)
    return pl.pallas_call(
        kernel,
        out_shape=(out, out),
        in_specs=[pl.BlockSpec(memory_space=pltpu.SMEM)] + [vmem] * 4 + [hbm] * 9,
        out_specs=(vmem, vmem),
        scratch_shapes=[pltpu.VMEM(w.shape, BF16) for w in weights]
        + [
            pltpu.VMEM((8, 24, 128), F32), pltpu.VMEM((8, 24, 128), F32), pltpu.VMEM((8, 24, 128), F32),
            pltpu.VMEM((8, 16, 128), BF16),
            pltpu.VMEM((64, 128), F32), pltpu.VMEM((64, 128), F32), pltpu.VMEM((64, 128), F32),
            pltpu.VMEM((8, 16, 128), F32), pltpu.VMEM((8, 16, 128), F32), pltpu.VMEM((8, 16, 128), F32),
            pltpu.VMEM((8, 8, 128), F32),
            pltpu.VMEM((8, 8, 128), F32),
            pltpu.VMEM((8, 128), F32), pltpu.VMEM((8, 8, 128), F32), pltpu.VMEM((8, 8, 128), F32),
            pltpu.VMEM((8, 16, BLOCK), BF16), pltpu.VMEM((8, 16, BLOCK), BF16), pltpu.VMEM((8, 16, BLOCK), BF16),
            pltpu.VMEM((8, 16, 256), BF16),
            pltpu.VMEM((8, 8, 128), F32),
            pltpu.SemaphoreType.DMA((9,)),
            pltpu.SemaphoreType.DMA((13,)),
            pltpu.SemaphoreType.DMA((13,)),
        ],
        compiler_params=pltpu.CompilerParams(
            collective_id=0, has_side_effects=True, vmem_limit_bytes=63 * 1024 * 1024
        ),
    )(lengths, tokens, attn_gain.reshape(1, 128), ffn_gain.reshape(1, 128), jnp.asarray(freq), *weights)


def solution(mesh):
    return jax.shard_map(
        body,
        mesh=mesh,
        in_specs=(
            P(None, None, "ctx"),
            P(),
            P("ctx"),
            P("ctx"),
            P("ctx", "kvh"),
            P("ctx", "kvh"),
            P("ctx", "kvh"),
            P("kvh", "ctx"),
            P("ctx", "kvh"),
            P("ctx", "kvh"),
            P("kvh", "ctx"),
            P(None, "ctx", "kvh", None),
            P(None, "ctx", "kvh", None),
        ),
        out_specs=(P(None, None, "ctx"), P(None, None, "ctx")),
        check_vma=False,
    )
```

time: 979 us -> 66.6 us (0.07)
  blocking collectives: 739 us -> 0 us
  waiting for transfers between devices: 183 us -> 0 us
  Pallas kernels: 0 us -> 63.9 us
  other arithmetic: 20.9 us -> 0 us
  between operations: 14 us -> 0.65 us
  matrix products: 10.5 us -> 0 us
    psum x5 -> x0, blocking collectives: 536 us -> none  [the longest x2 497 us: body(): lax.psum((sq_local, q_part, k_part, v_part), 'ctx')]
    all_gather x4 -> x0, blocking collectives: 203 us -> none  [merged(): pieces = jax.tree.map(lambda part: lax.all_gather(part, axis), value)]
    psum x1 -> x0, waiting for transfers between devices: 183 us -> none  [body(): sq_ffn, gate_sum, up_sum = lax.psum((sq_mid, gate_part, up_part), 'ctx')]
    pallas_call x0 -> x1, Pallas kernels: none -> 63.9 us  [body(): pl.pallas_call(kernel, out_shape=(out, out), in_specs=[pl.BlockSpec(memor...]
    dot_general x21 -> x0, matrix products: 10.5 us -> none  [the longest x2 1.71 us: body(): up_part = jnp.dot(xh, w_up, preferred_element_type=jnp.float32)]
    add x127 -> x0, other arithmetic: 10.3 us -> none  [the longest x126 10.3 us: combine_parts(): acc_a * factor_a[..., None] + acc_b * factor_b[..., None]]
  transfers between devices with their start and end apart: 3 -> 0, of which waited for: 1 -> 0; matrix products, arithmetic and copies ran while one was open for 0% -> 0% of each run, Pallas kernels for 0% -> 0%
where the time goes in v1:
time: 66.6 us; the launch traced here: 66.5 us
  Pallas kernels  63.9 us (96%)
  local copies, waits for them, and re-layouts  1.89 us (3%)
    pallas_call x1, Pallas kernels, body(): pl.pallas_call(kernel, out_shape=(out, out), in_specs=[pl.BlockSpec(memor...  63.9 us
    unnamed x6, local copies, waits for them, and re-layouts  1.89 us

profile of v1, /device:TPU:1, one launch (start us, length us, event | category | flops | bytes accessed | tf_op | source)
XLA Modules:
  0.0 66.5 jit_solution(15300928921102458421)
XLA Ops:
  0.6 63.9 %shard_map.149 = (bf16[2,4,128]{2,1,0:T(4,128)(2,1)}, bf16[2,4,128]{2,1,0:T(4,128)(2,1)}) custom-call(s32[4]{0:T(128)} %lengths.1, bf16[2,4,128]{2,1,0:T(4,128)(2,1)} %tokens.1, bf16[1,128]{1,0:T(2,128)(2,1)} %bitcast.6, bf16[1,128]{1,0:T(2,128)(2,1)} %bitcast.7, f32[1,128]{1,0:T(1,128)} %constant.2.clone.freq, bf16[128,1024]{1,0:T(8,128)(2,1)} %h_q.1, ...), custom_call_target="tpu_custom_call" | custom-call | tf_op jit(solution)/shard_map/pallas_call | solution.py:324
  64.6 0.0 copy-start.1
  64.6 0.7 copy-done.1
  65.2 0.0 copy-start
  65.2 0.6 copy.18
  65.8 0.1 copy-done
  65.9 0.6 copy.19
Async XLA Ops:
  64.6 0.7 %copy-start.1 = (bf16[2,4,128]{2,1,0:T(4,128)(2,1)S(1)}, bf16[2,4,128]{2,1,0:T(4,128)(2,1)}, u32[]{:S(2)}) copy-start(bf16[2,4,128]{2,1,0:T(4,128)(2,1)} %get-tuple-element.4) | copy-start | bytes 6148
  65.2 0.7 copy-start

commit v2 on v1

v2 whole, which is shorter than its diff:
```python
import math

import jax
import jax.numpy as jnp
import numpy as np
from jax import lax
from jax.experimental import pallas as pl
from jax.experimental.pallas import tpu as pltpu
from jax.sharding import PartitionSpec as P

MESH = pl.DeviceIdType.MESH
D = 8192
EPS = 1e-05
F32 = jnp.float32
BF16 = jnp.bfloat16
FAR_FIRST = (4, 3, 5, 2, 6, 1, 7)
TILES = 28
BLOCK = 512
QKV_RS, QKV_AR, K_MOVE, V_MOVE, ATT_RS, ATT_AR, ATT_AG, OUT_AR, SQ_RS, FFN_RS, SQ_AR, FFN_AR, FFN_AG, DOWN_AR = range(14)


def total_of(ref, rows):
    parts = [ref[i, rows, :].astype(F32) for i in range(8)]
    return ((parts[0] + parts[1]) + (parts[2] + parts[3])) + (
        (parts[4] + parts[5]) + (parts[6] + parts[7])
    )


def row_of(column):
    lane = lax.broadcasted_iota(jnp.int32, (8, 128), 1)
    row = lax.broadcasted_iota(jnp.int32, (8, 128), 0)
    return jnp.sum(jnp.where(lane == row, column, 0.0), axis=0, keepdims=True)


def column_of(line):
    lane = lax.broadcasted_iota(jnp.int32, (8, 128), 1)
    row = lax.broadcasted_iota(jnp.int32, (8, 128), 0)
    return jnp.sum(jnp.where(lane == row, line, 0.0), axis=1, keepdims=True)


def merged(partials):
    lane = lax.broadcasted_iota(jnp.int32, (8, 128), 1)
    low = lane < 64
    peaks, totals = [], []
    for part in partials:
        both = part[8:16]
        turned = pltpu.roll(both, 64, 1)
        peaks.append(jnp.where(low, both, turned))
        totals.append(jnp.where(low, turned, both))
    peak = peaks[0]
    for other in peaks[1:]:
        peak = jnp.maximum(peak, other)
    total = jnp.zeros((8, 128), F32)
    summed = jnp.zeros((8, 128), F32)
    for part, one_peak, one_total in zip(partials, peaks, totals):
        factor = jnp.exp(one_peak - peak)
        total += factor * one_total
        summed += factor * part[0:8]
    return peak, total, summed


def kernel(
    h_lengths, h_tokens, h_attn_gain, h_ffn_gain, h_freq,
    h_q, h_k, h_v, h_o, h_gate, h_up, h_down, h_kc, h_vc,
    out_ref,
    lengths, tokens, attn_gain, ffn_gain, freq,
    w_q, w_k, w_v, w_o, w_gate, w_up, w_down, k_c, v_c,
    s_qkv, r_qkv, r_qkv2,
    s_att, r_att, r_att2, r_attn,
    r_out,
    s_sq, r_sq, r_sq2,
    s_ffn, r_ffn, r_ffn2, r_hid,
    r_down,
    load_sem, send_sem, recv_sem,
):
    ctx = lax.axis_index("ctx")
    kvh = lax.axis_index("kvh")
    xc = lax.rem(ctx, 8)
    z = ctx // 8
    x = xc // 2
    c = lax.rem(xc, 2)

    def xc_peer(d):
        to = lax.rem(xc + d, 8)
        return to, (z * 8 + to, kvh)

    def z_peer(d):
        return (lax.rem(z + d, 8) * 8 + xc, kvh)

    def y_peer(d):
        return (ctx, lax.rem(kvh + d, 8))

    other_core = (z * 8 + x * 2 + (1 - c), kvh)

    def send(src, dst, stage, peer):
        pltpu.make_async_remote_copy(
            src_ref=src, dst_ref=dst, send_sem=send_sem.at[stage], recv_sem=recv_sem.at[stage],
            device_id=peer, device_id_type=MESH,
        ).start()

    def arrived(ref, stage):
        pltpu.make_async_copy(ref, ref, recv_sem.at[stage]).wait()

    barrier = pltpu.get_barrier_semaphore()
    for d in FAR_FIRST:
        pl.semaphore_signal(barrier, inc=1, device_id=xc_peer(d)[1], device_id_type=MESH)
    loads = {}
    for i, (name, src, dst) in enumerate(
        (
            ("tokens", h_tokens, tokens), ("attn_gain", h_attn_gain, attn_gain),
            ("q", h_q, w_q), ("k", h_k, w_k), ("v", h_v, w_v),
            ("lengths", h_lengths, lengths), ("freq", h_freq, freq), ("ffn_gain", h_ffn_gain, ffn_gain),
            ("kc", h_kc.at[x], k_c.at[x]), ("vc", h_vc.at[x], v_c.at[x]),
            ("o", h_o, w_o), ("gate", h_gate, w_gate), ("up", h_up, w_up), ("down", h_down, w_down),
        )
    ):
        loads[name] = pltpu.make_async_copy(src, dst, load_sem.at[i])
        loads[name].start()
    for d in FAR_FIRST:
        for peer in (z_peer(d), y_peer(d)):
            pl.semaphore_signal(barrier, inc=1, device_id=peer, device_id_type=MESH)

    loads["tokens"].wait()
    loads["attn_gain"].wait()
    hid = jnp.concatenate([tokens[0], tokens[1]], axis=0).astype(F32)
    sq = jnp.broadcast_to(jnp.sum(hid * hid, axis=1, keepdims=True), (8, 128))
    xg = (hid * attn_gain[...].astype(F32)).astype(BF16)
    for name in ("q", "k", "v"):
        loads[name].wait()
    q_part = jnp.dot(xg, w_q[...], preferred_element_type=F32)
    k_part = jnp.dot(xg, w_k[...], preferred_element_type=F32)
    v_part = jnp.dot(xg, w_v[...], preferred_element_type=F32)
    for s in range(2):
        rows = slice(s * 4, s * 4 + 4)
        for h in range(8):
            s_qkv[pl.ds(s * 8 + h, 4, stride=24), :] = q_part[rows, h * 128 : (h + 1) * 128]
        s_qkv[pl.ds(16 + s, 4, stride=24), :] = k_part[rows]
        s_qkv[pl.ds(18 + s, 4, stride=24), :] = v_part[rows]
        s_qkv[pl.ds(20 + s, 4, stride=24), :] = sq[rows]
    r_qkv[xc, 0:22, :] = s_qkv[pl.ds(pl.multiple_of(x * 24, 8), 22), :]

    pl.semaphore_wait(barrier, 21)
    for d in FAR_FIRST:
        to, peer = xc_peer(d)
        send(
            s_qkv.at[pl.ds(pl.multiple_of((to // 2) * 24, 8), 22)], r_qkv.at[xc, pl.ds(0, 22)], QKV_RS, peer
        )
    for d in (2, 1, 3):
        to = lax.rem(x + d, 4)
        peer = (z * 8 + to * 2 + c, kvh)
        send(h_kc.at[to], k_c.at[x], K_MOVE, peer)
        send(h_vc.at[to], v_c.at[x], V_MOVE, peer)

    loads["lengths"].wait()
    loads["freq"].wait()
    step8 = lax.broadcasted_iota(jnp.int32, (8, 128), 0)
    lane = lax.broadcasted_iota(jnp.int32, (8, 128), 1)
    length = lengths[x]
    angle = (length + step8).astype(F32) * freq[...]
    cosine = jnp.cos(angle)
    sine = jnp.sin(angle)
    sine = jnp.where(lane < 64, -sine, sine)

    arrived(r_qkv.at[pl.ds(0, 7), pl.ds(0, 22)], QKV_RS)
    r_qkv2[z, 0:22, :] = total_of(r_qkv, pl.ds(0, 22))
    for d in FAR_FIRST:
        mine = r_qkv2.at[z, pl.ds(0, 22)]
        send(mine, mine, QKV_AR, z_peer(d))
    arrived(r_qkv2.at[pl.ds(0, 7), pl.ds(0, 22)], QKV_AR)
    whole = total_of(r_qkv2, pl.ds(0, 22))
    queries, new_keys, new_values = [], [], []
    for s in range(2):
        scale = lax.rsqrt(whole[20 + s : 21 + s] / D + EPS)

        def rotary(a):
            return a * cosine[s : s + 1] + pltpu.roll(a, 64, 1) * sine[s : s + 1]

        queries.append(rotary(whole[s * 8 : s * 8 + 8] * scale).astype(BF16))
        key = jnp.broadcast_to(whole[16 + s : 17 + s] * scale, (8, 128))
        new_keys.append(rotary(key).astype(BF16).astype(F32))
        value = jnp.broadcast_to(whole[18 + s : 19 + s] * scale, (8, 128))
        new_values.append(value.astype(BF16).astype(F32))
    both_steps = jnp.concatenate(queries, axis=0)
    loads["kc"].wait()
    loads["vc"].wait()
    arrived(k_c.at[pl.ds(0, 3)], K_MOVE)

    scores, valid = [], []
    for i in range(4):
        scores.append(
            lax.dot_general(both_steps, k_c[i], (((1,), (1,)), ((), ())), preferred_element_type=F32)
            / math.sqrt(128)
        )
        first = (z * 8 + i * 2 + c) * 256
        valid.append(first + lax.broadcasted_iota(jnp.int32, (16, 256), 1) < length)
    scores = jnp.concatenate(scores, axis=1)
    valid = jnp.concatenate(valid, axis=1)
    scores = jnp.where(valid, scores, -1e30)
    peak = jnp.max(scores, axis=1, keepdims=True)
    weights = jnp.where(valid, jnp.exp(scores - peak), 0.0)
    total = jnp.sum(weights, axis=1, keepdims=True)
    weights = weights.astype(BF16)
    arrived(v_c.at[pl.ds(0, 3)], V_MOVE)
    acc = jnp.zeros((16, 128), F32)
    for i in range(4):
        acc += jnp.dot(weights[:, i * 256 : (i + 1) * 256], v_c[i], preferred_element_type=F32)
    both = jnp.where(lax.broadcasted_iota(jnp.int32, (16, 128), 1) < 64, peak, total)
    for s in range(2):
        rows = slice(s * 8, s * 8 + 8)
        s_att[s] = jnp.concatenate([acc[rows], both[rows]], axis=0)
    send(s_att.at[1 - c], r_att.at[0], ATT_RS, other_core)

    q_mine = jnp.where(c == 0, queries[0].astype(F32), queries[1].astype(F32))
    fresh = [jnp.sum(q_mine * key, axis=1, keepdims=True) / math.sqrt(128) for key in new_keys]
    f_first = jnp.broadcast_to(fresh[0], (8, 128))
    f_second = jnp.where(c == 1, jnp.broadcast_to(fresh[1], (8, 128)), -1e30)

    arrived(r_att.at[0], ATT_RS)
    peak, total, summed = merged([s_att[c], r_att[0]])
    r_att2[z, 0:8, :] = summed
    r_att2[z, 8:16, :] = jnp.where(lane < 64, peak, total)
    for d in FAR_FIRST:
        send(r_att2.at[z], r_att2.at[z], ATT_AR, z_peer(d))
    loads["o"].wait()
    arrived(r_att2.at[pl.ds(0, 7)], ATT_AR)
    peak, total, summed = merged([r_att2[i] for i in range(8)])
    top = jnp.maximum(peak, jnp.maximum(f_first, f_second))
    factor = jnp.exp(peak - top)
    e_first = jnp.exp(f_first - top)
    e_second = jnp.where(c == 1, jnp.exp(f_second - top), 0.0)
    total = total * factor + e_first + e_second
    summed = (
        summed * factor
        + e_first.astype(BF16).astype(F32) * new_values[0]
        + e_second.astype(BF16).astype(F32) * new_values[1]
    )
    mine = r_attn.at[pl.ds(pl.multiple_of((c * 4 + x) * 8, 8), 8)]
    mine[...] = summed / total
    for d in FAR_FIRST:
        send(mine, mine, ATT_AG, xc_peer(d)[1])
    arrived(r_attn.at[pl.ds(0, 56)], ATT_AG)

    attn = jnp.concatenate([r_attn[pl.ds(h, 8, stride=8), :] for h in range(8)], axis=1).astype(BF16)
    r_out[kvh] = jnp.dot(attn, w_o[...], preferred_element_type=F32)
    for d in FAR_FIRST:
        send(r_out.at[kvh], r_out.at[kvh], OUT_AR, y_peer(d))
    for name in ("gate", "up", "ffn_gain"):
        loads[name].wait()
    arrived(r_out.at[pl.ds(0, 7)], OUT_AR)
    attended = total_of(r_out, pl.ds(0, 8))
    x_mid = hid + attended
    s_sq[...] = jnp.broadcast_to(row_of(jnp.sum(x_mid * x_mid, axis=1, keepdims=True)), (8, 128))
    r_sq[xc] = s_sq[...]
    for d in FAR_FIRST:
        send(s_sq.at[pl.ds(0, 1)], r_sq.at[xc, pl.ds(0, 1)], SQ_RS, xc_peer(d)[1])

    xh = (x_mid * ffn_gain[...].astype(F32)).astype(BF16)
    for d in FAR_FIRST + (0,):
        to, peer = xc_peer(d)
        start = pl.multiple_of(((to // 2) * 7 + lax.rem(to, 2) * 3) * 128, 128)
        gate = jnp.dot(xh, w_gate[:, pl.ds(start, BLOCK)], preferred_element_type=F32)
        up = jnp.dot(xh, w_up[:, pl.ds(start, BLOCK)], preferred_element_type=F32)
        both = jnp.concatenate([gate, up], axis=0).astype(BF16)
        if d:
            s_ffn[to] = both
            send(s_ffn.at[to], r_ffn.at[xc], FFN_RS, peer)
        else:
            r_ffn[xc] = both
    out_ref[0] = attended[0:4].astype(BF16)
    out_ref[1] = attended[4:8].astype(BF16)
    arrived(r_sq.at[pl.ds(0, 7), pl.ds(0, 1)], SQ_RS)
    r_sq2[z, 0:1, :] = total_of(r_sq, pl.ds(0, 1))
    for d in FAR_FIRST:
        mine = r_sq2.at[z, pl.ds(0, 1)]
        send(mine, mine, SQ_AR, z_peer(d))
    arrived(r_ffn.at[pl.ds(0, 7)], FFN_RS)
    r_ffn2[z] = total_of(r_ffn, pl.ds(0, 16)).astype(BF16)
    for d in FAR_FIRST:
        send(r_ffn2.at[z], r_ffn2.at[z], FFN_AR, z_peer(d))
    arrived(r_sq2.at[pl.ds(0, 7), pl.ds(0, 1)], SQ_AR)
    scale = lax.rsqrt(column_of(total_of(r_sq2, pl.ds(0, 1))) / D + EPS)
    loads["down"].wait()
    arrived(r_ffn2.at[pl.ds(0, 7)], FFN_AR)
    both = total_of(r_ffn2, pl.ds(0, 16))
    gate = both[0:8] * scale
    hidden = gate / (1.0 + jnp.exp(-gate)) * (both[8:16] * scale)
    r_hid[xc] = jnp.concatenate([hidden[:, 0:256], hidden[:, 256:512]], axis=0).astype(BF16)
    for d in FAR_FIRST:
        send(r_hid.at[xc], r_hid.at[xc], FFN_AG, xc_peer(d)[1])
    arrived(r_hid.at[pl.ds(0, 7)], FFN_AG)

    pieces = []
    for j in range(8):
        piece = r_hid[j].astype(F32)
        if j % 2 == 0:
            pieces.append(piece[0:8])
        else:
            pieces.append(piece[0:8, 128:256])
        pieces.append(piece[8:16])
    r_down[kvh] = jnp.dot(
        jnp.concatenate(pieces, axis=1).astype(BF16), w_down[...], preferred_element_type=F32
    )
    for d in FAR_FIRST:
        send(r_down.at[kvh], r_down.at[kvh], DOWN_AR, y_peer(d))
    sent = (
        (r_qkv.at[pl.ds(0, 7), pl.ds(0, 22)], (QKV_RS, QKV_AR)),
        (k_c.at[pl.ds(0, 3)], (K_MOVE, V_MOVE)),
        (r_att.at[0], (ATT_RS,)),
        (r_att2.at[pl.ds(0, 7)], (ATT_AR,)),
        (r_attn.at[pl.ds(0, 56)], (ATT_AG,)),
        (r_out.at[pl.ds(0, 7)], (OUT_AR,)),
        (r_sq.at[pl.ds(0, 7), pl.ds(0, 1)], (SQ_RS, SQ_AR)),
        (r_ffn.at[pl.ds(0, 7)], (FFN_RS, FFN_AR)),
        (r_hid.at[pl.ds(0, 7)], (FFN_AG,)),
        (r_down.at[pl.ds(0, 7)], (DOWN_AR,)),
    )
    for ref, stages in sent:
        for stage in stages:
            pltpu.make_async_copy(ref, ref, send_sem.at[stage]).wait()
    arrived(r_down.at[pl.ds(0, 7)], DOWN_AR)
    layer = x_mid + total_of(r_down, pl.ds(0, 8))
    out_ref[2] = layer[0:4].astype(BF16)
    out_ref[3] = layer[4:8].astype(BF16)


def body(tokens, lengths, attn_gain, ffn_gain, w_q, w_k, w_v, w_o, w_gate, w_up, w_down, k_cache, v_cache):
    half = np.arange(64, dtype=np.float64)
    freq = np.tile(500000.0 ** (-2.0 * half / 128.0), 2).astype(np.float32)[None]
    k_cache = k_cache.reshape(4, 256, 128)
    v_cache = v_cache.reshape(4, 256, 128)
    hbm = pl.BlockSpec(memory_space=pltpu.HBM)
    small = (tokens, attn_gain.reshape(1, 128), ffn_gain.reshape(1, 128), jnp.asarray(freq))
    weights = (w_q, w_k, w_v, w_o, w_gate, w_up, w_down, k_cache, v_cache)
    both = pl.pallas_call(
        kernel,
        out_shape=pltpu.VMEM((4, 4, 128), BF16),
        in_specs=[hbm] * 14,
        out_specs=pl.BlockSpec(memory_space=pltpu.VMEM),
        scratch_shapes=[pltpu.SMEM((4,), jnp.int32)]
        + [pltpu.VMEM(a.shape, a.dtype) for a in small + weights]
        + [
            pltpu.VMEM((96, 128), F32), pltpu.VMEM((8, 24, 128), F32), pltpu.VMEM((8, 24, 128), F32),
            pltpu.VMEM((2, 16, 128), F32), pltpu.VMEM((1, 16, 128), F32), pltpu.VMEM((8, 16, 128), F32),
            pltpu.VMEM((64, 128), F32),
            pltpu.VMEM((8, 8, 128), F32),
            pltpu.VMEM((8, 128), F32), pltpu.VMEM((8, 8, 128), F32), pltpu.VMEM((8, 8, 128), F32),
            pltpu.VMEM((8, 16, BLOCK), BF16), pltpu.VMEM((8, 16, BLOCK), BF16), pltpu.VMEM((8, 16, BLOCK), BF16),
            pltpu.VMEM((8, 16, 256), BF16),
            pltpu.VMEM((8, 8, 128), F32),
            pltpu.SemaphoreType.DMA((14,)),
            pltpu.SemaphoreType.DMA((14,)),
            pltpu.SemaphoreType.DMA((14,)),
        ],
        compiler_params=pltpu.CompilerParams(
            collective_id=0, has_side_effects=True, vmem_limit_bytes=60 * 1024 * 1024
        ),
    )(*[pltpu.with_memory_space_constraint(a, pltpu.HBM) for a in (lengths, *small, *weights)])
    return both[0:2], both[2:4]


def solution(mesh):
    return jax.shard_map(
        body,
        mesh=mesh,
        in_specs=(
            P(None, None, "ctx"),
            P(),
            P("ctx"),
            P("ctx"),
            P("ctx", "kvh"),
            P("ctx", "kvh"),
            P("ctx", "kvh"),
            P("kvh", "ctx"),
            P("ctx", "kvh"),
            P("ctx", "kvh"),
            P("kvh", "ctx"),
            P(None, "ctx", "kvh", None),
            P(None, "ctx", "kvh", None),
        ),
        out_specs=(P(None, None, "ctx"), P(None, None, "ctx")),
        check_vma=False,
    )
```

time: 66.6 us -> 58.6 us (0.88)
  Pallas kernels: 63.9 us -> 57.3 us
  local copies, waits for them, and re-layouts: 1.89 us -> 0.59 us
    pallas_call x1, Pallas kernels: 63.9 us -> 57.3 us  [body(): pl.pallas_call(kernel, out_shape=pltpu.VMEM((4, 4, 128), BF16), in_specs=...]
    unnamed x6 -> x0, local copies, waits for them, and re-layouts: 1.89 us -> none
where the time goes in v2:
time: 58.6 us; the launch traced here: 58.5 us
  Pallas kernels  57.3 us (98%)
  between operations  0.64 us (1%)
  local copies, waits for them, and re-layouts  0.59 us (1%)
    pallas_call x1, Pallas kernels, body(): pl.pallas_call(kernel, out_shape=pltpu.VMEM((4, 4, 128), BF16), in_specs=...  57.3 us

profile of v2, /device:TPU:1, one launch (start us, length us, event | category | flops | bytes accessed | tf_op | source)
XLA Modules:
  0.0 58.5 jit_solution(17213776264698256888)
XLA Ops:
  0.6 57.3 %shard_map.149 = bf16[4,4,128]{2,1,0:T(4,128)(2,1)S(1)} custom-call(s32[4]{0:T(128)} %h_lengths.1, bf16[2,4,128]{2,1,0:T(4,128)(2,1)} %h_tokens.1, bf16[1,128]{1,0:T(2,128)(2,1)} %bitcast.6, bf16[1,128]{1,0:T(2,128)(2,1)} %bitcast.7, f32[1,128]{1,0:T(1,128)} %constant.2.clone.h_freq, bf16[128,1024]{1,0:T(8,128)(2,1)} %h_q.1, bf16[128,128]{1,0:T(8,128)(2,1)} %h_k.1, ...), custom_call_target="tpu_custom_call" | custom-call | tf_op jit(solution)/shard_map/pallas_call | solution.py:334
  57.9 0.6 %fusion = (bf16[2,4,128]{2,1,0:T(4,128)(2,1)}, bf16[2,4,128]{2,1,0:T(4,128)(2,1)}) fusion(bf16[4,4,128]{2,1,0:T(4,128)(2,1)S(1)} %shard_map.149), kind=kLoop, calls=%fused_computation | loop fusion | bytes 8192 | tf_op jit(solution)/shard_map/slice | solution.py:358

commit v3 on v2

--- a/solution.py
+++ b/solution.py
@@ -16,7 +16,7 @@
 FAR_FIRST = (4, 3, 5, 2, 6, 1, 7)
 TILES = 28
 BLOCK = 512
-QKV_RS, QKV_AR, K_MOVE, V_MOVE, ATT_RS, ATT_AR, ATT_AG, OUT_AR, SQ_RS, FFN_RS, SQ_AR, FFN_AR, FFN_AG, DOWN_AR = range(14)
+QKV_RS, QKV_AR, K_MOVE, V_MOVE, ATT_AR, ATT_AG, OUT_AR, SQ_RS, FFN_RS, SQ_AR, FFN_AR, FFN_AG, DOWN_AR = range(13)
 
 
 def total_of(ref, rows):
@@ -38,25 +38,16 @@
     return jnp.sum(jnp.where(lane == row, line, 0.0), axis=1, keepdims=True)
 
 
-def merged(partials):
-    lane = lax.broadcasted_iota(jnp.int32, (8, 128), 1)
-    low = lane < 64
-    peaks, totals = [], []
-    for part in partials:
-        both = part[8:16]
-        turned = pltpu.roll(both, 64, 1)
-        peaks.append(jnp.where(low, both, turned))
-        totals.append(jnp.where(low, turned, both))
-    peak = peaks[0]
-    for other in peaks[1:]:
-        peak = jnp.maximum(peak, other)
-    total = jnp.zeros((8, 128), F32)
-    summed = jnp.zeros((8, 128), F32)
-    for part, one_peak, one_total in zip(partials, peaks, totals):
-        factor = jnp.exp(one_peak - peak)
-        total += factor * one_total
-        summed += factor * part[0:8]
-    return peak, total, summed
+def merged(ref):
+    lines = ref[pl.ds(8, 16, stride=16), :]
+    head = lax.broadcasted_iota(jnp.int32, (16, 128), 1) < 8
+    peak = jnp.max(lines, axis=0, keepdims=True)
+    factors = jnp.where(head, jnp.exp(jnp.where(head, lines - peak, 0.0)), 0.0)
+    total = jnp.sum(factors * pltpu.roll(lines, 120, 1), axis=0, keepdims=True)
+    terms = [column_of(factors[i : i + 1]) * ref[i * 16 : i * 16 + 8, :] for i in range(16)]
+    while len(terms) > 1:
+        terms = [a + b for a, b in zip(terms[0::2], terms[1::2])]
+    return column_of(peak), column_of(total), terms[0]
 
 
 def kernel(
@@ -66,7 +57,7 @@
     lengths, tokens, attn_gain, ffn_gain, freq,
     w_q, w_k, w_v, w_o, w_gate, w_up, w_down, k_c, v_c,
     s_qkv, r_qkv, r_qkv2,
-    s_att, r_att, r_att2, r_attn,
+    s_att, r_att, r_attn,
     r_out,
     s_sq, r_sq, r_sq2,
     s_ffn, r_ffn, r_ffn2, r_hid,
@@ -90,7 +81,14 @@
     def y_peer(d):
         return (ctx, lax.rem(kvh + d, 8))
 
-    other_core = (z * 8 + x * 2 + (1 - c), kvh)
+    def zc_peers():
+        for d in FAR_FIRST:
+            yield c, (lax.rem(z + d, 8) * 8 + xc, kvh)
+            yield 1 - c, (lax.rem(z + d, 8) * 8 + x * 2 + (1 - c), kvh)
+        yield 1 - c, (z * 8 + x * 2 + (1 - c), kvh)
+
+    def z_other(d):
+        return (lax.rem(z + d, 8) * 8 + x * 2 + (1 - c), kvh)
 
     def send(src, dst, stage, peer):
         pltpu.make_async_remote_copy(
@@ -117,7 +115,7 @@
         loads[name] = pltpu.make_async_copy(src, dst, load_sem.at[i])
         loads[name].start()
     for d in FAR_FIRST:
-        for peer in (z_peer(d), y_peer(d)):
+        for peer in (z_peer(d), z_other(d), y_peer(d)):
             pl.semaphore_signal(barrier, inc=1, device_id=peer, device_id_type=MESH)
 
     loads["tokens"].wait()
@@ -130,26 +128,25 @@
     q_part = jnp.dot(xg, w_q[...], preferred_element_type=F32)
     k_part = jnp.dot(xg, w_k[...], preferred_element_type=F32)
     v_part = jnp.dot(xg, w_v[...], preferred_element_type=F32)
-    for s in range(2):
-        rows = slice(s * 4, s * 4 + 4)
-        for h in range(8):
-            s_qkv[pl.ds(s * 8 + h, 4, stride=24), :] = q_part[rows, h * 128 : (h + 1) * 128]
-        s_qkv[pl.ds(16 + s, 4, stride=24), :] = k_part[rows]
-        s_qkv[pl.ds(18 + s, 4, stride=24), :] = v_part[rows]
-        s_qkv[pl.ds(20 + s, 4, stride=24), :] = sq[rows]
-    r_qkv[xc, 0:22, :] = s_qkv[pl.ds(pl.multiple_of(x * 24, 8), 22), :]
-
-    pl.semaphore_wait(barrier, 21)
+    for h in range(8):
+        s_qkv[pl.ds(h, 8, stride=16), :] = q_part[:, h * 128 : (h + 1) * 128]
+    s_qkv[pl.ds(8, 8, stride=16), :] = k_part
+    s_qkv[pl.ds(9, 8, stride=16), :] = v_part
+    s_qkv[pl.ds(10, 8, stride=16), :] = sq
+
+    def row_block(to):
+        return pl.ds(pl.multiple_of((lax.rem(to, 2) * 4 + to // 2) * 16, 16), 11)
+
+    r_qkv[xc, 0:11, :] = s_qkv[row_block(xc), :]
+
+    pl.semaphore_wait(barrier, 28)
     for d in FAR_FIRST:
         to, peer = xc_peer(d)
-        send(
-            s_qkv.at[pl.ds(pl.multiple_of((to // 2) * 24, 8), 22)], r_qkv.at[xc, pl.ds(0, 22)], QKV_RS, peer
-        )
+        send(s_qkv.at[row_block(to)], r_qkv.at[xc, pl.ds(0, 11)], QKV_RS, peer)
     for d in (2, 1, 3):
         to = lax.rem(x + d, 4)
         peer = (z * 8 + to * 2 + c, kvh)
         send(h_kc.at[to], k_c.at[x], K_MOVE, peer)
-        send(h_vc.at[to], v_c.at[x], V_MOVE, peer)
 
     loads["lengths"].wait()
     loads["freq"].wait()
@@ -161,24 +158,30 @@
     sine = jnp.sin(angle)
     sine = jnp.where(lane < 64, -sine, sine)
 
-    arrived(r_qkv.at[pl.ds(0, 7), pl.ds(0, 22)], QKV_RS)
-    r_qkv2[z, 0:22, :] = total_of(r_qkv, pl.ds(0, 22))
-    for d in FAR_FIRST:
-        mine = r_qkv2.at[z, pl.ds(0, 22)]
-        send(mine, mine, QKV_AR, z_peer(d))
-    arrived(r_qkv2.at[pl.ds(0, 7), pl.ds(0, 22)], QKV_AR)
-    whole = total_of(r_qkv2, pl.ds(0, 22))
+    arrived(r_qkv.at[pl.ds(0, 7), pl.ds(0, 11)], QKV_RS)
+    r_qkv2[z * 2 + c, 0:11, :] = total_of(r_qkv, pl.ds(0, 11))
+    mine = r_qkv2.at[z * 2 + c, pl.ds(0, 11)]
+    for _, peer in zc_peers():
+        send(mine, mine, QKV_AR, peer)
+    for d in (2, 1, 3):
+        to = lax.rem(x + d, 4)
+        send(h_vc.at[to], v_c.at[x], V_MOVE, (z * 8 + to * 2 + c, kvh))
+    arrived(r_qkv2.at[pl.ds(0, 15), pl.ds(0, 11)], QKV_AR)
     queries, new_keys, new_values = [], [], []
     for s in range(2):
-        scale = lax.rsqrt(whole[20 + s : 21 + s] / D + EPS)
+        parts = [r_qkv2[i * 2 + s, 0:11, :] for i in range(8)]
+        while len(parts) > 1:
+            parts = [a + b for a, b in zip(parts[0::2], parts[1::2])]
+        whole = parts[0]
+        scale = lax.rsqrt(whole[10:11] / D + EPS)
 
         def rotary(a):
             return a * cosine[s : s + 1] + pltpu.roll(a, 64, 1) * sine[s : s + 1]
 
-        queries.append(rotary(whole[s * 8 : s * 8 + 8] * scale).astype(BF16))
-        key = jnp.broadcast_to(whole[16 + s : 17 + s] * scale, (8, 128))
+        queries.append(rotary(whole[0:8] * scale).astype(BF16))
+        key = jnp.broadcast_to(whole[8:9] * scale, (8, 128))
         new_keys.append(rotary(key).astype(BF16).astype(F32))
-        value = jnp.broadcast_to(whole[18 + s : 19 + s] * scale, (8, 128))
+        value = jnp.broadcast_to(whole[9:10] * scale, (8, 128))
         new_values.append(value.astype(BF16).astype(F32))
     both_steps = jnp.concatenate(queries, axis=0)
     loads["kc"].wait()
@@ -204,26 +207,24 @@
     acc = jnp.zeros((16, 128), F32)
     for i in range(4):
         acc += jnp.dot(weights[:, i * 256 : (i + 1) * 256], v_c[i], preferred_element_type=F32)
-    both = jnp.where(lax.broadcasted_iota(jnp.int32, (16, 128), 1) < 64, peak, total)
     for s in range(2):
         rows = slice(s * 8, s * 8 + 8)
-        s_att[s] = jnp.concatenate([acc[rows], both[rows]], axis=0)
-    send(s_att.at[1 - c], r_att.at[0], ATT_RS, other_core)
+        s_att[s, 0:8, :] = acc[rows]
+        line = jnp.where(lane == step8, peak[rows], jnp.where(lane == step8 + 8, total[rows], 0.0))
+        s_att[s, 8:9, :] = jnp.sum(line, axis=0, keepdims=True)
+    slot = pl.ds(pl.multiple_of((z * 2 + c) * 16, 16), 9)
+    r_att[slot, :] = s_att[c, 0:9, :]
+    for core, peer in zc_peers():
+        send(s_att.at[core, pl.ds(0, 9)], r_att.at[slot], ATT_AR, peer)
 
     q_mine = jnp.where(c == 0, queries[0].astype(F32), queries[1].astype(F32))
     fresh = [jnp.sum(q_mine * key, axis=1, keepdims=True) / math.sqrt(128) for key in new_keys]
     f_first = jnp.broadcast_to(fresh[0], (8, 128))
     f_second = jnp.where(c == 1, jnp.broadcast_to(fresh[1], (8, 128)), -1e30)
 
-    arrived(r_att.at[0], ATT_RS)
-    peak, total, summed = merged([s_att[c], r_att[0]])
-    r_att2[z, 0:8, :] = summed
-    r_att2[z, 8:16, :] = jnp.where(lane < 64, peak, total)
-    for d in FAR_FIRST:
-        send(r_att2.at[z], r_att2.at[z], ATT_AR, z_peer(d))
     loads["o"].wait()
-    arrived(r_att2.at[pl.ds(0, 7)], ATT_AR)
-    peak, total, summed = merged([r_att2[i] for i in range(8)])
+    arrived(r_att.at[pl.ds(0, 15 * 9)], ATT_AR)
+    peak, total, summed = merged(r_att)
     top = jnp.maximum(peak, jnp.maximum(f_first, f_second))
     factor = jnp.exp(peak - top)
     e_first = jnp.exp(f_first - top)
@@ -303,10 +304,10 @@
     for d in FAR_FIRST:
         send(r_down.at[kvh], r_down.at[kvh], DOWN_AR, y_peer(d))
     sent = (
-        (r_qkv.at[pl.ds(0, 7), pl.ds(0, 22)], (QKV_RS, QKV_AR)),
+        (r_qkv.at[pl.ds(0, 7), pl.ds(0, 11)], (QKV_RS,)),
+        (r_qkv2.at[pl.ds(0, 15), pl.ds(0, 11)], (QKV_AR,)),
         (k_c.at[pl.ds(0, 3)], (K_MOVE, V_MOVE)),
-        (r_att.at[0], (ATT_RS,)),
-        (r_att2.at[pl.ds(0, 7)], (ATT_AR,)),
+        (r_att.at[pl.ds(0, 15 * 9)], (ATT_AR,)),
         (r_attn.at[pl.ds(0, 56)], (ATT_AG,)),
         (r_out.at[pl.ds(0, 7)], (OUT_AR,)),
         (r_sq.at[pl.ds(0, 7), pl.ds(0, 1)], (SQ_RS, SQ_AR)),
@@ -339,8 +340,8 @@
         scratch_shapes=[pltpu.SMEM((4,), jnp.int32)]
         + [pltpu.VMEM(a.shape, a.dtype) for a in small + weights]
         + [
-            pltpu.VMEM((96, 128), F32), pltpu.VMEM((8, 24, 128), F32), pltpu.VMEM((8, 24, 128), F32),
-            pltpu.VMEM((2, 16, 128), F32), pltpu.VMEM((1, 16, 128), F32), pltpu.VMEM((8, 16, 128), F32),
+            pltpu.VMEM((128, 128), F32), pltpu.VMEM((8, 16, 128), F32), pltpu.VMEM((16, 16, 128), F32),
+            pltpu.VMEM((2, 16, 128), F32), pltpu.VMEM((256, 128), F32),
             pltpu.VMEM((64, 128), F32),
             pltpu.VMEM((8, 8, 128), F32),
             pltpu.VMEM((8, 128), F32), pltpu.VMEM((8, 8, 128), F32), pltpu.VMEM((8, 8, 128), F32),
@@ -348,8 +349,8 @@
             pltpu.VMEM((8, 16, 256), BF16),
             pltpu.VMEM((8, 8, 128), F32),
             pltpu.SemaphoreType.DMA((14,)),
-            pltpu.SemaphoreType.DMA((14,)),
-            pltpu.SemaphoreType.DMA((14,)),
+            pltpu.SemaphoreType.DMA((13,)),
+            pltpu.SemaphoreType.DMA((13,)),
         ],
         compiler_params=pltpu.CompilerParams(
             collective_id=0, has_side_effects=True, vmem_limit_bytes=60 * 1024 * 1024

time: 58.6 us -> 56.6 us (0.966)
  Pallas kernels: 57.3 us -> 55.2 us
    pallas_call x1, Pallas kernels: 57.3 us -> 55.2 us  [body(): pl.pallas_call(kernel, out_shape=pltpu.VMEM((4, 4, 128), BF16), in_specs=...]
where the time goes in v3:
time: 56.6 us; the launch traced here: 56.5 us
  Pallas kernels  55.2 us (98%)
  between operations  0.64 us (1%)
  local copies, waits for them, and re-layouts  0.59 us (1%)
    pallas_call x1, Pallas kernels, body(): pl.pallas_call(kernel, out_shape=pltpu.VMEM((4, 4, 128), BF16), in_specs=...  55.2 us

profile of v3, /device:TPU:1, one launch (start us, length us, event | category | flops | bytes accessed | tf_op | source)
XLA Modules:
  0.0 56.5 jit_solution(16379335659142025054)
XLA Ops:
  0.6 55.2 %shard_map.149 = bf16[4,4,128]{2,1,0:T(4,128)(2,1)S(1)} custom-call(s32[4]{0:T(128)} %h_lengths.1, bf16[2,4,128]{2,1,0:T(4,128)(2,1)} %h_tokens.1, bf16[1,128]{1,0:T(2,128)(2,1)} %bitcast.6, bf16[1,128]{1,0:T(2,128)(2,1)} %bitcast.7, f32[1,128]{1,0:T(1,128)} %constant.2.clone.h_freq, bf16[128,1024]{1,0:T(8,128)(2,1)} %h_q.1, bf16[128,128]{1,0:T(8,128)(2,1)} %h_k.1, ...), custom_call_target="tpu_custom_call" | custom-call | tf_op jit(solution)/shard_map/pallas_call | solution.py:335
  55.9 0.6 %fusion = (bf16[2,4,128]{2,1,0:T(4,128)(2,1)}, bf16[2,4,128]{2,1,0:T(4,128)(2,1)}) fusion(bf16[4,4,128]{2,1,0:T(4,128)(2,1)S(1)} %shard_map.149), kind=kLoop, calls=%fused_computation | loop fusion | bytes 8192 | tf_op jit(solution)/shard_map/slice | solution.py:359

commit v4 on v3

--- a/solution.py
+++ b/solution.py
@@ -14,9 +14,10 @@
 F32 = jnp.float32
 BF16 = jnp.bfloat16
 FAR_FIRST = (4, 3, 5, 2, 6, 1, 7)
+RING = ((2, 0), (2, 1), (1, 0), (3, 0), (1, 1), (3, 1), (0, 1))
 TILES = 28
 BLOCK = 512
-QKV_RS, QKV_AR, K_MOVE, V_MOVE, ATT_AR, ATT_AG, OUT_AR, SQ_RS, FFN_RS, SQ_AR, FFN_AR, FFN_AG, DOWN_AR = range(13)
+QKV_RS, QKV_AR, K_MOVE, V_MOVE, ATT_AR, ATT_AG, OUT_AR, FFN_RS, FFN_AR, FFN_AG, DOWN_AR = range(11)
 
 
 def total_of(ref, rows):
@@ -26,16 +27,26 @@
     )
 
 
-def row_of(column):
-    lane = lax.broadcasted_iota(jnp.int32, (8, 128), 1)
-    row = lax.broadcasted_iota(jnp.int32, (8, 128), 0)
-    return jnp.sum(jnp.where(lane == row, column, 0.0), axis=0, keepdims=True)
-
-
 def column_of(line):
     lane = lax.broadcasted_iota(jnp.int32, (8, 128), 1)
     row = lax.broadcasted_iota(jnp.int32, (8, 128), 0)
     return jnp.sum(jnp.where(lane == row, line, 0.0), axis=1, keepdims=True)
+
+
+def with_square(both, square, core):
+    lane = lax.broadcasted_iota(jnp.int32, (16, 128), 1)
+    high = square.astype(BF16).astype(F32)
+    terms = jnp.concatenate([high, square - high], axis=0)
+    first = jnp.where((core == 1) & (lane < 64), terms, both[:, 0:128])
+    last = jnp.where((core == 0) & (lane >= 64), terms, both[:, 384:512])
+    return jnp.concatenate([first, both[:, 128:384], last], axis=1)
+
+
+def square_of(both, core):
+    lane = lax.broadcasted_iota(jnp.int32, (16, 128), 1)
+    tile = jnp.where(core == 1, both[:, 0:128], pltpu.roll(both[:, 384:512], 64, 1))
+    tile = jnp.where(lane < 64, tile, pltpu.roll(tile, 64, 1))
+    return tile[0:8] + tile[8:16]
 
 
 def merged(ref):
@@ -59,10 +70,9 @@
     s_qkv, r_qkv, r_qkv2,
     s_att, r_att, r_attn,
     r_out,
-    s_sq, r_sq, r_sq2,
     s_ffn, r_ffn, r_ffn2, r_hid,
     r_down,
-    load_sem, send_sem, recv_sem,
+    load_sem, send_sem, recv_sem, near_sem,
 ):
     ctx = lax.axis_index("ctx")
     kvh = lax.axis_index("kvh")
@@ -71,12 +81,16 @@
     x = xc // 2
     c = lax.rem(xc, 2)
 
-    def xc_peer(d):
-        to = lax.rem(xc + d, 8)
+    def xc_peer(step):
+        dx, dc = step
+        to = lax.rem(x + dx, 4) * 2 + lax.rem(c + dc, 2)
         return to, (z * 8 + to, kvh)
 
     def z_peer(d):
         return (lax.rem(z + d, 8) * 8 + xc, kvh)
+
+    def z_other(d):
+        return (lax.rem(z + d, 8) * 8 + x * 2 + (1 - c), kvh)
 
     def y_peer(d):
         return (ctx, lax.rem(kvh + d, 8))
@@ -87,9 +101,6 @@
             yield 1 - c, (lax.rem(z + d, 8) * 8 + x * 2 + (1 - c), kvh)
         yield 1 - c, (z * 8 + x * 2 + (1 - c), kvh)
 
-    def z_other(d):
-        return (lax.rem(z + d, 8) * 8 + x * 2 + (1 - c), kvh)
-
     def send(src, dst, stage, peer):
         pltpu.make_async_remote_copy(
             src_ref=src, dst_ref=dst, send_sem=send_sem.at[stage], recv_sem=recv_sem.at[stage],
@@ -100,8 +111,17 @@
         pltpu.make_async_copy(ref, ref, recv_sem.at[stage]).wait()
 
     barrier = pltpu.get_barrier_semaphore()
-    for d in FAR_FIRST:
-        pl.semaphore_signal(barrier, inc=1, device_id=xc_peer(d)[1], device_id_type=MESH)
+    near = [peer(d) for peer in (z_peer, z_other, y_peer) for d in (1, 7)]
+    for peer in near + [xc_peer(d)[1] for d in RING]:
+        pl.semaphore_signal(barrier, inc=1, device_id=peer, device_id_type=MESH)
+
+    def tell(i, peer_at):
+        for d in (1, 7):
+            pl.semaphore_signal(near_sem.at[i], inc=1, device_id=peer_at(d), device_id_type=MESH)
+
+    def heard(i):
+        pl.semaphore_wait(near_sem.at[i], 2)
+
     loads = {}
     for i, (name, src, dst) in enumerate(
         (
@@ -114,10 +134,6 @@
     ):
         loads[name] = pltpu.make_async_copy(src, dst, load_sem.at[i])
         loads[name].start()
-    for d in FAR_FIRST:
-        for peer in (z_peer(d), z_other(d), y_peer(d)):
-            pl.semaphore_signal(barrier, inc=1, device_id=peer, device_id_type=MESH)
-
     loads["tokens"].wait()
     loads["attn_gain"].wait()
     hid = jnp.concatenate([tokens[0], tokens[1]], axis=0).astype(F32)
@@ -139,14 +155,18 @@
 
     r_qkv[xc, 0:11, :] = s_qkv[row_block(xc), :]
 
-    pl.semaphore_wait(barrier, 28)
-    for d in FAR_FIRST:
+    pl.semaphore_wait(barrier, 13)
+    tell(0, z_peer)
+    for d in RING:
         to, peer = xc_peer(d)
         send(s_qkv.at[row_block(to)], r_qkv.at[xc, pl.ds(0, 11)], QKV_RS, peer)
     for d in (2, 1, 3):
         to = lax.rem(x + d, 4)
         peer = (z * 8 + to * 2 + c, kvh)
         send(h_kc.at[to], k_c.at[x], K_MOVE, peer)
+
+    heard(0)
+    tell(1, z_peer)
 
     loads["lengths"].wait()
     loads["freq"].wait()
@@ -158,6 +178,10 @@
     sine = jnp.sin(angle)
     sine = jnp.where(lane < 64, -sine, sine)
 
+    heard(1)
+    tell(2, z_peer)
+    heard(2)
+    tell(3, y_peer)
     arrived(r_qkv.at[pl.ds(0, 7), pl.ds(0, 11)], QKV_RS)
     r_qkv2[z * 2 + c, 0:11, :] = total_of(r_qkv, pl.ds(0, 11))
     mine = r_qkv2.at[z * 2 + c, pl.ds(0, 11)]
@@ -166,6 +190,8 @@
     for d in (2, 1, 3):
         to = lax.rem(x + d, 4)
         send(h_vc.at[to], v_c.at[x], V_MOVE, (z * 8 + to * 2 + c, kvh))
+    heard(3)
+    tell(4, y_peer)
     arrived(r_qkv2.at[pl.ds(0, 15), pl.ds(0, 11)], QKV_AR)
     queries, new_keys, new_values = [], [], []
     for s in range(2):
@@ -222,6 +248,9 @@
     f_first = jnp.broadcast_to(fresh[0], (8, 128))
     f_second = jnp.where(c == 1, jnp.broadcast_to(fresh[1], (8, 128)), -1e30)
 
+    heard(4)
+    tell(5, y_peer)
+    heard(5)
     loads["o"].wait()
     arrived(r_att.at[pl.ds(0, 15 * 9)], ATT_AR)
     peak, total, summed = merged(r_att)
@@ -237,7 +266,7 @@
     )
     mine = r_attn.at[pl.ds(pl.multiple_of((c * 4 + x) * 8, 8), 8)]
     mine[...] = summed / total
-    for d in FAR_FIRST:
+    for d in RING:
         send(mine, mine, ATT_AG, xc_peer(d)[1])
     arrived(r_attn.at[pl.ds(0, 56)], ATT_AG)
 
@@ -250,54 +279,47 @@
     arrived(r_out.at[pl.ds(0, 7)], OUT_AR)
     attended = total_of(r_out, pl.ds(0, 8))
     x_mid = hid + attended
-    s_sq[...] = jnp.broadcast_to(row_of(jnp.sum(x_mid * x_mid, axis=1, keepdims=True)), (8, 128))
-    r_sq[xc] = s_sq[...]
-    for d in FAR_FIRST:
-        send(s_sq.at[pl.ds(0, 1)], r_sq.at[xc, pl.ds(0, 1)], SQ_RS, xc_peer(d)[1])
+    square = jnp.broadcast_to(jnp.sum(x_mid * x_mid, axis=1, keepdims=True), (8, 128))
 
     xh = (x_mid * ffn_gain[...].astype(F32)).astype(BF16)
-    for d in FAR_FIRST + (0,):
+    for d in RING + ((0, 0),):
         to, peer = xc_peer(d)
         start = pl.multiple_of(((to // 2) * 7 + lax.rem(to, 2) * 3) * 128, 128)
         gate = jnp.dot(xh, w_gate[:, pl.ds(start, BLOCK)], preferred_element_type=F32)
         up = jnp.dot(xh, w_up[:, pl.ds(start, BLOCK)], preferred_element_type=F32)
-        both = jnp.concatenate([gate, up], axis=0).astype(BF16)
-        if d:
+        both = with_square(jnp.concatenate([gate, up], axis=0), square, lax.rem(to, 2)).astype(BF16)
+        if d != (0, 0):
             s_ffn[to] = both
             send(s_ffn.at[to], r_ffn.at[xc], FFN_RS, peer)
         else:
             r_ffn[xc] = both
     out_ref[0] = attended[0:4].astype(BF16)
     out_ref[1] = attended[4:8].astype(BF16)
-    arrived(r_sq.at[pl.ds(0, 7), pl.ds(0, 1)], SQ_RS)
-    r_sq2[z, 0:1, :] = total_of(r_sq, pl.ds(0, 1))
-    for d in FAR_FIRST:
-        mine = r_sq2.at[z, pl.ds(0, 1)]
-        send(mine, mine, SQ_AR, z_peer(d))
     arrived(r_ffn.at[pl.ds(0, 7)], FFN_RS)
-    r_ffn2[z] = total_of(r_ffn, pl.ds(0, 16)).astype(BF16)
+    both = total_of(r_ffn, pl.ds(0, 16))
+    r_ffn2[z] = with_square(both, square_of(both, c), c).astype(BF16)
     for d in FAR_FIRST:
         send(r_ffn2.at[z], r_ffn2.at[z], FFN_AR, z_peer(d))
-    arrived(r_sq2.at[pl.ds(0, 7), pl.ds(0, 1)], SQ_AR)
-    scale = lax.rsqrt(column_of(total_of(r_sq2, pl.ds(0, 1))) / D + EPS)
     loads["down"].wait()
     arrived(r_ffn2.at[pl.ds(0, 7)], FFN_AR)
     both = total_of(r_ffn2, pl.ds(0, 16))
+    scale = lax.rsqrt(square_of(both, c) / D + EPS)[:, 0:1]
     gate = both[0:8] * scale
     hidden = gate / (1.0 + jnp.exp(-gate)) * (both[8:16] * scale)
+    unit = lax.broadcasted_iota(jnp.int32, (8, BLOCK), 1)
+    hidden = jnp.where((unit >= c * 64) & (unit < 448 + c * 64), hidden, 0.0)
     r_hid[xc] = jnp.concatenate([hidden[:, 0:256], hidden[:, 256:512]], axis=0).astype(BF16)
-    for d in FAR_FIRST:
+    for d in RING:
         send(r_hid.at[xc], r_hid.at[xc], FFN_AG, xc_peer(d)[1])
     arrived(r_hid.at[pl.ds(0, 7)], FFN_AG)
 
     pieces = []
-    for j in range(8):
-        piece = r_hid[j].astype(F32)
-        if j % 2 == 0:
-            pieces.append(piece[0:8])
-        else:
-            pieces.append(piece[0:8, 128:256])
-        pieces.append(piece[8:16])
+    for j in range(4):
+        even = r_hid[2 * j].astype(F32)
+        odd = r_hid[2 * j + 1].astype(F32)
+        pieces += [
+            even[0:8], even[8:16, 0:128], even[8:16, 128:256] + odd[0:8, 0:128], odd[0:8, 128:256], odd[8:16]
+        ]
     r_down[kvh] = jnp.dot(
         jnp.concatenate(pieces, axis=1).astype(BF16), w_down[...], preferred_element_type=F32
     )
@@ -310,7 +332,6 @@
         (r_att.at[pl.ds(0, 15 * 9)], (ATT_AR,)),
         (r_attn.at[pl.ds(0, 56)], (ATT_AG,)),
         (r_out.at[pl.ds(0, 7)], (OUT_AR,)),
-        (r_sq.at[pl.ds(0, 7), pl.ds(0, 1)], (SQ_RS, SQ_AR)),
         (r_ffn.at[pl.ds(0, 7)], (FFN_RS, FFN_AR)),
         (r_hid.at[pl.ds(0, 7)], (FFN_AG,)),
         (r_down.at[pl.ds(0, 7)], (DOWN_AR,)),
@@ -344,13 +365,13 @@
             pltpu.VMEM((2, 16, 128), F32), pltpu.VMEM((256, 128), F32),
             pltpu.VMEM((64, 128), F32),
             pltpu.VMEM((8, 8, 128), F32),
-            pltpu.VMEM((8, 128), F32), pltpu.VMEM((8, 8, 128), F32), pltpu.VMEM((8, 8, 128), F32),
             pltpu.VMEM((8, 16, BLOCK), BF16), pltpu.VMEM((8, 16, BLOCK), BF16), pltpu.VMEM((8, 16, BLOCK), BF16),
             pltpu.VMEM((8, 16, 256), BF16),
             pltpu.VMEM((8, 8, 128), F32),
             pltpu.SemaphoreType.DMA((14,)),
-            pltpu.SemaphoreType.DMA((13,)),
-            pltpu.SemaphoreType.DMA((13,)),
+            pltpu.SemaphoreType.DMA((11,)),
+            pltpu.SemaphoreType.DMA((11,)),
+            pltpu.SemaphoreType.REGULAR((6,)),
         ],
         compiler_params=pltpu.CompilerParams(
             collective_id=0, has_side_effects=True, vmem_limit_bytes=60 * 1024 * 1024

time: 56.6 us -> 55.6 us (0.982)
  Pallas kernels: 55.2 us -> 54.2 us
    pallas_call x1, Pallas kernels: 55.2 us -> 54.2 us  [body(): pl.pallas_call(kernel, out_shape=pltpu.VMEM((4, 4, 128), BF16), in_specs=...]
where the time goes in v4:
time: 55.6 us; the launch traced here: 55.5 us
  Pallas kernels  54.2 us (97%)
  between operations  0.64 us (1%)
  local copies, waits for them, and re-layouts  0.59 us (1%)
    pallas_call x1, Pallas kernels, body(): pl.pallas_call(kernel, out_shape=pltpu.VMEM((4, 4, 128), BF16), in_specs=...  54.2 us

profile of v4, /device:TPU:1, one launch (start us, length us, event | category | flops | bytes accessed | tf_op | source)
XLA Modules:
  0.0 55.5 jit_solution(14840726139629285390)
XLA Ops:
  0.6 54.2 %shard_map.149 = bf16[4,4,128]{2,1,0:T(4,128)(2,1)S(1)} custom-call(s32[4]{0:T(128)} %h_lengths.1, bf16[2,4,128]{2,1,0:T(4,128)(2,1)} %h_tokens.1, bf16[1,128]{1,0:T(2,128)(2,1)} %bitcast.6, bf16[1,128]{1,0:T(2,128)(2,1)} %bitcast.7, f32[1,128]{1,0:T(1,128)} %constant.2.clone.h_freq, bf16[128,1024]{1,0:T(8,128)(2,1)} %h_q.1, bf16[128,128]{1,0:T(8,128)(2,1)} %h_k.1, ...), custom_call_target="tpu_custom_call" | custom-call | tf_op jit(solution)/shard_map/pallas_call | solution.py:356
  54.9 0.6 %fusion = (bf16[2,4,128]{2,1,0:T(4,128)(2,1)}, bf16[2,4,128]{2,1,0:T(4,128)(2,1)}) fusion(bf16[4,4,128]{2,1,0:T(4,128)(2,1)S(1)} %shard_map.149), kind=kLoop, calls=%fused_computation | loop fusion | bytes 8192 | tf_op jit(solution)/shard_map/slice | solution.py:380

commit v5 on v4

--- a/solution.py
+++ b/solution.py
@@ -111,16 +111,16 @@
         pltpu.make_async_copy(ref, ref, recv_sem.at[stage]).wait()
 
     barrier = pltpu.get_barrier_semaphore()
-    near = [peer(d) for peer in (z_peer, z_other, y_peer) for d in (1, 7)]
+    near = [z_peer(d) for d in (2, 6, 1, 7)] + [z_other(d) for d in (2, 6, 1, 7)] + [y_peer(1), y_peer(7)]
     for peer in near + [xc_peer(d)[1] for d in RING]:
         pl.semaphore_signal(barrier, inc=1, device_id=peer, device_id_type=MESH)
 
-    def tell(i, peer_at):
-        for d in (1, 7):
+    def tell(i, peer_at, steps=(1, 7)):
+        for d in steps:
             pl.semaphore_signal(near_sem.at[i], inc=1, device_id=peer_at(d), device_id_type=MESH)
 
-    def heard(i):
-        pl.semaphore_wait(near_sem.at[i], 2)
+    def heard(i, count=2):
+        pl.semaphore_wait(near_sem.at[i], count)
 
     loads = {}
     for i, (name, src, dst) in enumerate(
@@ -155,8 +155,8 @@
 
     r_qkv[xc, 0:11, :] = s_qkv[row_block(xc), :]
 
-    pl.semaphore_wait(barrier, 13)
-    tell(0, z_peer)
+    pl.semaphore_wait(barrier, 17)
+    tell(0, z_peer, (2, 6, 1, 7))
     for d in RING:
         to, peer = xc_peer(d)
         send(s_qkv.at[row_block(to)], r_qkv.at[xc, pl.ds(0, 11)], QKV_RS, peer)
@@ -165,8 +165,7 @@
         peer = (z * 8 + to * 2 + c, kvh)
         send(h_kc.at[to], k_c.at[x], K_MOVE, peer)
 
-    heard(0)
-    tell(1, z_peer)
+    heard(0, 4)
 
     loads["lengths"].wait()
     loads["freq"].wait()
@@ -178,9 +177,6 @@
     sine = jnp.sin(angle)
     sine = jnp.where(lane < 64, -sine, sine)
 
-    heard(1)
-    tell(2, z_peer)
-    heard(2)
     tell(3, y_peer)
     arrived(r_qkv.at[pl.ds(0, 7), pl.ds(0, 11)], QKV_RS)
     r_qkv2[z * 2 + c, 0:11, :] = total_of(r_qkv, pl.ds(0, 11))

time: 55.6 us -> 54.9 us (0.987)
  Pallas kernels: 54.2 us -> 53.5 us
    pallas_call x1, Pallas kernels: 54.2 us -> 53.5 us  [body(): pl.pallas_call(kernel, out_shape=pltpu.VMEM((4, 4, 128), BF16), in_specs=...]
where the time goes in v5:
time: 54.9 us; the launch traced here: 54.8 us
  Pallas kernels  53.5 us (97%)
  between operations  0.64 us (1%)
  local copies, waits for them, and re-layouts  0.59 us (1%)
    pallas_call x1, Pallas kernels, body(): pl.pallas_call(kernel, out_shape=pltpu.VMEM((4, 4, 128), BF16), in_specs=...  53.5 us

profile of v5, /device:TPU:1, one launch (start us, length us, event | category | flops | bytes accessed | tf_op | source)
XLA Modules:
  0.0 54.8 jit_solution(15890089467584833857)
XLA Ops:
  0.6 53.5 %shard_map.149 = bf16[4,4,128]{2,1,0:T(4,128)(2,1)S(1)} custom-call(s32[4]{0:T(128)} %h_lengths.1, bf16[2,4,128]{2,1,0:T(4,128)(2,1)} %h_tokens.1, bf16[1,128]{1,0:T(2,128)(2,1)} %bitcast.6, bf16[1,128]{1,0:T(2,128)(2,1)} %bitcast.7, f32[1,128]{1,0:T(1,128)} %constant.2.clone.h_freq, bf16[128,1024]{1,0:T(8,128)(2,1)} %h_q.1, bf16[128,128]{1,0:T(8,128)(2,1)} %h_k.1, ...), custom_call_target="tpu_custom_call" | custom-call | tf_op jit(solution)/shard_map/pallas_call | solution.py:352
  54.2 0.6 %fusion = (bf16[2,4,128]{2,1,0:T(4,128)(2,1)}, bf16[2,4,128]{2,1,0:T(4,128)(2,1)}) fusion(bf16[4,4,128]{2,1,0:T(4,128)(2,1)S(1)} %shard_map.149), kind=kLoop, calls=%fused_computation | loop fusion | bytes 8192 | tf_op jit(solution)/shard_map/slice | solution.py:376

commit v6 on v5

--- a/solution.py
+++ b/solution.py
@@ -357,9 +357,9 @@
         scratch_shapes=[pltpu.SMEM((4,), jnp.int32)]
         + [pltpu.VMEM(a.shape, a.dtype) for a in small + weights]
         + [
-            pltpu.VMEM((128, 128), F32), pltpu.VMEM((8, 16, 128), F32), pltpu.VMEM((16, 16, 128), F32),
-            pltpu.VMEM((2, 16, 128), F32), pltpu.VMEM((256, 128), F32),
-            pltpu.VMEM((64, 128), F32),
+            pltpu.VMEM((144, 128), F32), pltpu.VMEM((8, 16, 128), F32), pltpu.VMEM((16, 16, 128), F32),
+            pltpu.VMEM((2, 16, 128), F32), pltpu.VMEM((272, 128), F32),
+            pltpu.VMEM((72, 128), F32),
             pltpu.VMEM((8, 8, 128), F32),
             pltpu.VMEM((8, 16, BLOCK), BF16), pltpu.VMEM((8, 16, BLOCK), BF16), pltpu.VMEM((8, 16, BLOCK), BF16),
             pltpu.VMEM((8, 16, 256), BF16),

time: 54.9 us -> 54.9 us (level)
  no operation moved by 1% of the time
where the time goes in v6:
time: 54.9 us; the launch traced here: 54.8 us
  Pallas kernels  53.5 us (97%)
  between operations  0.64 us (1%)
  local copies, waits for them, and re-layouts  0.59 us (1%)
    pallas_call x1, Pallas kernels, body(): pl.pallas_call(kernel, out_shape=pltpu.VMEM((4, 4, 128), BF16), in_specs=...  53.5 us

profile of v6, /device:TPU:1, one launch (start us, length us, event | category | flops | bytes accessed | tf_op | source)
XLA Modules:
  0.0 54.8 jit_solution(2358526474826422196)
XLA Ops:
  0.6 53.5 %shard_map.149 = bf16[4,4,128]{2,1,0:T(4,128)(2,1)S(1)} custom-call(s32[4]{0:T(128)} %h_lengths.1, bf16[2,4,128]{2,1,0:T(4,128)(2,1)} %h_tokens.1, bf16[1,128]{1,0:T(2,128)(2,1)} %bitcast.6, bf16[1,128]{1,0:T(2,128)(2,1)} %bitcast.7, f32[1,128]{1,0:T(1,128)} %constant.2.clone.h_freq, bf16[128,1024]{1,0:T(8,128)(2,1)} %h_q.1, bf16[128,128]{1,0:T(8,128)(2,1)} %h_k.1, ...), custom_call_target="tpu_custom_call" | custom-call | tf_op jit(solution)/shard_map/pallas_call | solution.py:352
  54.2 0.6 %fusion = (bf16[2,4,128]{2,1,0:T(4,128)(2,1)}, bf16[2,4,128]{2,1,0:T(4,128)(2,1)}) fusion(bf16[4,4,128]{2,1,0:T(4,128)(2,1)S(1)} %shard_map.149), kind=kLoop, calls=%fused_computation | loop fusion | bytes 8192 | tf_op jit(solution)/shard_map/slice | solution.py:376

commit v7 on v6

--- a/solution.py
+++ b/solution.py
@@ -165,6 +165,9 @@
         peer = (z * 8 + to * 2 + c, kvh)
         send(h_kc.at[to], k_c.at[x], K_MOVE, peer)
 
+    for d in (2, 1, 3):
+        to = lax.rem(x + d, 4)
+        send(h_vc.at[to], v_c.at[x], V_MOVE, (z * 8 + to * 2 + c, kvh))
     heard(0, 4)
 
     loads["lengths"].wait()
@@ -183,9 +186,6 @@
     mine = r_qkv2.at[z * 2 + c, pl.ds(0, 11)]
     for _, peer in zc_peers():
         send(mine, mine, QKV_AR, peer)
-    for d in (2, 1, 3):
-        to = lax.rem(x + d, 4)
-        send(h_vc.at[to], v_c.at[x], V_MOVE, (z * 8 + to * 2 + c, kvh))
     heard(3)
     tell(4, y_peer)
     arrived(r_qkv2.at[pl.ds(0, 15), pl.ds(0, 11)], QKV_AR)

time: 54.9 us -> 54.9 us (level)
  no operation moved by 1% of the time
where the time goes in v7:
time: 54.9 us; the launch traced here: 54.8 us
  Pallas kernels  53.5 us (97%)
  between operations  0.64 us (1%)
  local copies, waits for them, and re-layouts  0.59 us (1%)
    pallas_call x1, Pallas kernels, body(): pl.pallas_call(kernel, out_shape=pltpu.VMEM((4, 4, 128), BF16), in_specs=...  53.5 us

profile of v7, /device:TPU:1, one launch (start us, length us, event | category | flops | bytes accessed | tf_op | source)
XLA Modules:
  0.0 54.8 jit_solution(9614332512634835108)
XLA Ops:
  0.6 53.5 %shard_map.149 = bf16[4,4,128]{2,1,0:T(4,128)(2,1)S(1)} custom-call(s32[4]{0:T(128)} %h_lengths.1, bf16[2,4,128]{2,1,0:T(4,128)(2,1)} %h_tokens.1, bf16[1,128]{1,0:T(2,128)(2,1)} %bitcast.6, bf16[1,128]{1,0:T(2,128)(2,1)} %bitcast.7, f32[1,128]{1,0:T(1,128)} %constant.2.clone.h_freq, bf16[128,1024]{1,0:T(8,128)(2,1)} %h_q.1, bf16[128,128]{1,0:T(8,128)(2,1)} %h_k.1, ...), custom_call_target="tpu_custom_call" | custom-call | tf_op jit(solution)/shard_map/pallas_call | solution.py:352
  54.2 0.6 %fusion = (bf16[2,4,128]{2,1,0:T(4,128)(2,1)}, bf16[2,4,128]{2,1,0:T(4,128)(2,1)}) fusion(bf16[4,4,128]{2,1,0:T(4,128)(2,1)S(1)} %shard_map.149), kind=kLoop, calls=%fused_computation | loop fusion | bytes 8192 | tf_op jit(solution)/shard_map/slice | solution.py:376
